TPU v7x, 512 devices: a whole 4x4x16 slice. The times are simulated.
512 devices in a mesh: turb: 32 (over y, z_lo, core), age: 16 (over x, z_hi).
Axes of the slice: x: 4, y: 4, z: 16 (z_hi: 4, z_lo: 4; z = z_hi * 4 + z_lo), core: 2. Of those that a mesh axis runs over, the one named last changes fastest.
Arguments:
- positions: float32 [3, 192, 32768], P(None, 'turb', 'age'), may hold values from -6 to 6
- circulation: float32 [192, 32768], P('turb', 'age'), may hold values from -6 to 6
- send_lists: int32 [32, 16, 32, 6], P('turb', 'age'), may hold values from 0 to 95
- reader_slots: int32 [32, 16, 96, 8], P('turb', 'age'), may hold values from 0 to 191
- source_counts: int32 [32, 16, 96], P('turb', 'age'), may hold values from 1 to 8, as said below
- near_blocks: int32 [32, 16, 96, 4], P('turb', 'age'), may hold values from 0 to 95
Outputs:
- velocity: float32 [3, 192, 32768], P(None, 'turb', 'age')
- moved: float32 [3, 192, 32768], P(None, 'turb', 'age')
Inputs may be any that keep to these rules, and one draw needn't show every extreme that they name: `source_counts`: the number of remote sources listed for a reader tile; entries of reader_slots at or past it are unused.
All inputs are finite; a program needn't handle non-finite values.
Results may differ from a plain program's by a relative error of at most 0.0003.
Values sent between devices are 32-bit elements; how exact they have to be, the bound alone decides.
No kernel may reach another device: no remote copies, remote signals or barrier semaphores. Data moves between devices by JAX's collectives and lax.ppermute only.
A program may use at most 64 MiB of HBM per device.

v0:
```python
import jax
import jax.numpy as jnp
from jax import lax
from jax.sharding import PartitionSpec as P

SPAN = 64


time_step = 0.1
core_square = 0.25
inflow_speed = 1.0
inv_four_pi = 0.07957747154594767


def passed_along(value, axis, steps):
    count = lax.axis_size(axis)
    leading, last = (max(0, -steps), min(count, count - steps))
    return lax.ppermute(value, axis, [(source, source + steps) for source in range(leading, last)])


def induce(points, sources):
    apart_x = points[:, 0, :, None] - sources[:, 0, None, :]
    apart_y = points[:, 1, :, None] - sources[:, 1, None, :]
    apart_z = points[:, 2, :, None] - sources[:, 2, None, :]
    square = apart_x * apart_x + apart_y * apart_y + apart_z * apart_z + core_square
    weight = inv_four_pi * lax.rsqrt(square) / square
    strength_x = sources[:, 3, None, :]
    strength_y = sources[:, 4, None, :]
    strength_z = sources[:, 5, None, :]
    cross_x = strength_y * apart_z - strength_z * apart_y
    cross_y = strength_z * apart_x - strength_x * apart_z
    cross_z = strength_x * apart_y - strength_y * apart_x
    return jnp.stack(
        [
            jnp.sum(cross_x * weight, axis=2),
            jnp.sum(cross_y * weight, axis=2),
            jnp.sum(cross_z * weight, axis=2),
        ],
        axis=1,
    )


def body(positions, circulation, send_lists, reader_slots, source_counts, near_blocks):
    rows = positions.shape[1]
    width = positions.shape[2]
    tile = 2 * SPAN
    halves = width // tile
    tiles = rows * halves
    first_row = positions[:, :, :SPAN]
    next_row = passed_along(first_row, "age", -1)
    following = jnp.concatenate([positions[:, :, SPAN:], next_row], axis=2)
    column = lax.broadcasted_iota(jnp.int32, (1, 1, width), 2)
    at_end = (lax.axis_index("age") == lax.axis_size("age") - 1) & (column >= width - SPAN)
    segment = jnp.where(at_end, 0.0, following - positions)
    middle = positions + 0.5 * segment
    strength = circulation[None] * segment

    def to_blocks(field):
        comps = field.shape[0]
        return (
            field.reshape(comps, rows, halves, tile)
            .transpose(1, 2, 0, 3)
            .reshape(tiles, comps, tile)
        )

    sources = to_blocks(jnp.concatenate([middle, strength], axis=0))
    points = to_blocks(positions)
    peers = lax.axis_size("turb")
    everyone = lax.all_gather(sources, "turb", axis=0, tiled=True)
    all_lists = lax.all_gather(send_lists, "turb", axis=0, tiled=True)
    mine = lax.dynamic_index_in_dim(all_lists[:, 0], lax.axis_index("turb"), axis=1, keepdims=False)
    chosen = (jnp.arange(peers, dtype=jnp.int32)[:, None] * tiles + mine).reshape(-1)
    received = jnp.take(everyone, chosen, axis=0)
    slots = reader_slots[0, 0]
    counts = source_counts[0, 0]
    nearby = near_blocks[0, 0]
    total = jnp.zeros((tiles, 3, tile), jnp.float32)
    for step in range(nearby.shape[1]):
        total = total + induce(points, jnp.take(sources, nearby[:, step], axis=0))

    def far_step(index, running):
        slot = lax.dynamic_index_in_dim(slots, index, axis=1, keepdims=False)
        term = induce(points, jnp.take(received, slot, axis=0))
        return running + jnp.where((index < counts)[:, None, None], term, 0.0)

    total = lax.fori_loop(0, jnp.max(counts), far_step, total)
    velocity = total.reshape(rows, halves, 3, tile).transpose(2, 0, 1, 3).reshape(3, rows, width)
    inflow = jnp.array([inflow_speed, 0.0, 0.0], jnp.float32)[:, None, None]
    moved = positions + time_step * (velocity + inflow)
    return (velocity, moved)


def solution(mesh):
    in_specs = (
        P(None, "turb", "age"),
        P("turb", "age"),
        P("turb", "age", None, None),
        P("turb", "age", None, None),
        P("turb", "age", None),
        P("turb", "age", None, None),
    )
    out_specs = (P(None, "turb", "age"), P(None, "turb", "age"))
    return jax.shard_map(body, mesh=mesh, in_specs=in_specs, out_specs=out_specs, check_vma=False)
```

profile of v0, /device:TPU:131, one launch (start us, length us, event | category | flops | bytes accessed | tf_op | source)
XLA Modules:
  0.0 290.1 jit_solution(16845052113679158049)
XLA Ops:
  7.2 0.7 slice.136
  7.9 1.9 collective-permute-start
  9.9 1.0 slice.135
  10.9 6.9 %collective-permute-done = f32[3,6,64]{2,1,0:T(8,128)S(1)} collective-permute-done((f32[3,6,64]{2,1,0:T(8,128)S(1)}, f32[3,6,64]{2,1,0:T(8,128)S(1)}, u32[]{:S(2)}, u32[]{:S(2)}) %collective-permute-start) | collective-permute-done | bytes 4640 | tf_op jit(solution)/shard_map/ppermute | solution.py:18
  17.8 1.0 multiply_add_fusion.1
  18.9 0.8 reshape.93
  19.7 1.0 reshape.95
  21.0 45.8 %all_gather.6 = s32[32,1,32,6]{2,1,3,0:T(1,128)S(1)} all-gather(s32[1,1,32,6]{2,1,3,0:T(1,128)} %param.13), channel_id=1, replica_groups=mesh['turb'=32,'age'=16] {'turb'}, dimensions={0}, use_global_device_ids=true | all-gather | bytes 25344 | tf_op jit(solution)/shard_map/all_gather | solution.py:70
  66.7 3.7 %dynamic-slice_reduce_fusion = s32[32,6]{1,0:T(8,128)S(1)} fusion(s32[32,1,32,6]{2,1,3,0:T(1,128)S(1)} %all_gather.6, s32[]{:T(128)S(6)} %select_n.55), kind=kLoop, calls=%fused_computation.139 | loop fusion | bytes 1540 | tf_op jit(solution)/shard_map/jit(dynamic_index_in_dim)/dynamic_slice | solution.py:71
  70.6 1.3 reduce_max.9
  71.9 0.8 compare_and_fusion.2
  72.9 1.1 copy.19
  78.2 27.9 %fusion.39 = (f32[96,128]{1,0:T(8,128)S(1)}, f32[96,128]{1,0:T(8,128)S(1)}, f32[96,128]{1,0:T(8,128)S(1)}, f32[96,128]{1,0:T(8,128)S(1)}, f32[96,128]{1,0:T(8,128)S(1)}, /*index=5*/f32[96,128]{1,0:T(8,128)S(1)}) fusion(f32[96,128]{1,0:T(8,128)S(1)} %bitcast.132, f32[96,128]{1,0:T(8,128)S(1)} %bitcast.133, f32[96,128]{1,0:T(8,128)S(1)} %bitcast.134, ...), kind=kLoop, calls=%fused_computation.100 | loop fusion | flops 81715200 | bytes 1032192 | tf_op jit(solution)/shard_map/reduce_sum | solution.py:35
  106.2 27.7 %fusion.51 = (f32[96,128]{1,0:T(8,128)S(1)}, f32[96,128]{1,0:T(8,128)S(1)}, f32[96,128]{1,0:T(8,128)S(1)}, f32[96,128]{1,0:T(8,128)S(1)}, f32[96,128]{1,0:T(8,128)S(1)}, /*index=5*/f32[96,128]{1,0:T(8,128)S(1)}) fusion(f32[96,128]{1,0:T(8,128)S(1)} %bitcast.138, f32[96,128]{1,0:T(8,128)S(1)} %bitcast.139, f32[96,128]{1,0:T(8,128)S(1)} %bitcast.140, ...), kind=kLoop, calls=%fused_computation.112 | loop fusion | flops 81715200 | bytes 1032192 | tf_op jit(solution)/shard_map/reduce_sum | solution.py:35
  134.0 12.7 %copy.21 = f32[3072,6,128]{2,1,0:T(8,128)} copy(f32[3072,6,128]{2,0,1:T(8,128)} %all-gather.2.cloned.1.call-done) | data formatting | bytes 18874368 | tf_op jit(solution)/shard_map/all_gather | solution.py:69
  146.7 5.3 %gather_fusion.1 = f32[192,6,128]{2,1,0:T(8,128)S(1)} fusion(f32[3072,6,128]{2,1,0:T(8,128)} %copy.21, s32[1024]{0:T(1024)S(1)} %pad_clamp_fusion.1), kind=kCustom, calls=%fused_computation.5 | custom fusion | bytes 1180416 | tf_op jit(solution)/shard_map/jit(_take)/gather | solution.py:73
  152.2 130.2 %while.10 = (s32[]{:T(128)}, f32[96,3,128]{2,0,1:T(8,128)S(1)}, s32[]{:T(128)}, s32[96]{0:T(128)S(1)}, s32[96,8]{0,1:T(8,128)}, /*index=5*/f32[192,6,128]{2,1,0:...) while((s32[]{:T(128)}, f32[96,3,128]{2,0,1:T(8,128)S(1)}, s32[]{:T(128)}, ...), condition=%wide.region_17.19_spmd, body=%wide.region_13.18_spmd.sunk | while | flops 41080484 | bytes 3103127 | solution.py:86
  153.0 0.7 and_bitcast_fusion.2
  154.8 13.6 %fusion.74 = (f32[96,128]{1,0:T(8,128)S(1)}, f32[96,128]{1,0:T(8,128)S(1)}, f32[96,128]{1,0:T(8,128)S(1)}) fusion(f32[96,128]{1,0:T(8,128)S(1)} %bitcast.122, f32[96,128]{1,0:T(8,128)S(1)} %get-tuple-element.196, f32[96,128]{1,0:T(8,128)S(1)} %bitcast.123, f32[96,128]{1,0:T(8,128)S(1)} %bitcast.124, f32[96,128]{1,0:T(8,128)S(1)} %get-tuple-element.199, ...), kind=kLoop, calls=%fused_computation.17.clone.1 | loop fusion | flops 40857600 | bytes 589824 | tf_op jit(solution)/shard_map/while/body/reduce_sum | solution.py:35
  171.0 13.6 %fusion.74 = (f32[96,128]{1,0:T(8,128)S(1)}, f32[96,128]{1,0:T(8,128)S(1)}, f32[96,128]{1,0:T(8,128)S(1)}) fusion(f32[96,128]{1,0:T(8,128)S(1)} %bitcast.122, f32[96,128]{1,0:T(8,128)S(1)} %get-tuple-element.196, f32[96,128]{1,0:T(8,128)S(1)} %bitcast.123, f32[96,128]{1,0:T(8,128)S(1)} %bitcast.124, f32[96,128]{1,0:T(8,128)S(1)} %get-tuple-element.199, ...), kind=kLoop, calls=%fused_computation.17.clone.1 | loop fusion | flops 40857600 | bytes 589824 | tf_op jit(solution)/shard_map/while/body/reduce_sum | solution.py:35
  185.3 0.7 and_bitcast_fusion.2
  187.1 13.6 %fusion.74 = (f32[96,128]{1,0:T(8,128)S(1)}, f32[96,128]{1,0:T(8,128)S(1)}, f32[96,128]{1,0:T(8,128)S(1)}) fusion(f32[96,128]{1,0:T(8,128)S(1)} %bitcast.122, f32[96,128]{1,0:T(8,128)S(1)} %get-tuple-element.196, f32[96,128]{1,0:T(8,128)S(1)} %bitcast.123, f32[96,128]{1,0:T(8,128)S(1)} %bitcast.124, f32[96,128]{1,0:T(8,128)S(1)} %get-tuple-element.199, ...), kind=kLoop, calls=%fused_computation.17.clone.1 | loop fusion | flops 40857600 | bytes 589824 | tf_op jit(solution)/shard_map/while/body/reduce_sum | solution.py:35
  201.5 0.7 and_bitcast_fusion.2
  203.3 13.6 %fusion.74 = (f32[96,128]{1,0:T(8,128)S(1)}, f32[96,128]{1,0:T(8,128)S(1)}, f32[96,128]{1,0:T(8,128)S(1)}) fusion(f32[96,128]{1,0:T(8,128)S(1)} %bitcast.122, f32[96,128]{1,0:T(8,128)S(1)} %get-tuple-element.196, f32[96,128]{1,0:T(8,128)S(1)} %bitcast.123, f32[96,128]{1,0:T(8,128)S(1)} %bitcast.124, f32[96,128]{1,0:T(8,128)S(1)} %get-tuple-element.199, ...), kind=kLoop, calls=%fused_computation.17.clone.1 | loop fusion | flops 40857600 | bytes 589824 | tf_op jit(solution)/shard_map/while/body/reduce_sum | solution.py:35
  217.7 0.7 and_bitcast_fusion.2
  219.5 13.6 %fusion.74 = (f32[96,128]{1,0:T(8,128)S(1)}, f32[96,128]{1,0:T(8,128)S(1)}, f32[96,128]{1,0:T(8,128)S(1)}) fusion(f32[96,128]{1,0:T(8,128)S(1)} %bitcast.122, f32[96,128]{1,0:T(8,128)S(1)} %get-tuple-element.196, f32[96,128]{1,0:T(8,128)S(1)} %bitcast.123, f32[96,128]{1,0:T(8,128)S(1)} %bitcast.124, f32[96,128]{1,0:T(8,128)S(1)} %get-tuple-element.199, ...), kind=kLoop, calls=%fused_computation.17.clone.1 | loop fusion | flops 40857600 | bytes 589824 | tf_op jit(solution)/shard_map/while/body/reduce_sum | solution.py:35
  233.9 0.7 and_bitcast_fusion.2
  235.7 13.6 %fusion.74 = (f32[96,128]{1,0:T(8,128)S(1)}, f32[96,128]{1,0:T(8,128)S(1)}, f32[96,128]{1,0:T(8,128)S(1)}) fusion(f32[96,128]{1,0:T(8,128)S(1)} %bitcast.122, f32[96,128]{1,0:T(8,128)S(1)} %get-tuple-element.196, f32[96,128]{1,0:T(8,128)S(1)} %bitcast.123, f32[96,128]{1,0:T(8,128)S(1)} %bitcast.124, f32[96,128]{1,0:T(8,128)S(1)} %get-tuple-element.199, ...), kind=kLoop, calls=%fused_computation.17.clone.1 | loop fusion | flops 40857600 | bytes 589824 | tf_op jit(solution)/shard_map/while/body/reduce_sum | solution.py:35
  250.1 0.7 and_bitcast_fusion.2
  251.9 13.6 %fusion.74 = (f32[96,128]{1,0:T(8,128)S(1)}, f32[96,128]{1,0:T(8,128)S(1)}, f32[96,128]{1,0:T(8,128)S(1)}) fusion(f32[96,128]{1,0:T(8,128)S(1)} %bitcast.122, f32[96,128]{1,0:T(8,128)S(1)} %get-tuple-element.196, f32[96,128]{1,0:T(8,128)S(1)} %bitcast.123, f32[96,128]{1,0:T(8,128)S(1)} %bitcast.124, f32[96,128]{1,0:T(8,128)S(1)} %get-tuple-element.199, ...), kind=kLoop, calls=%fused_computation.17.clone.1 | loop fusion | flops 40857600 | bytes 589824 | tf_op jit(solution)/shard_map/while/body/reduce_sum | solution.py:35
  268.1 13.6 %fusion.74 = (f32[96,128]{1,0:T(8,128)S(1)}, f32[96,128]{1,0:T(8,128)S(1)}, f32[96,128]{1,0:T(8,128)S(1)}) fusion(f32[96,128]{1,0:T(8,128)S(1)} %bitcast.122, f32[96,128]{1,0:T(8,128)S(1)} %get-tuple-element.196, f32[96,128]{1,0:T(8,128)S(1)} %bitcast.123, f32[96,128]{1,0:T(8,128)S(1)} %bitcast.124, f32[96,128]{1,0:T(8,128)S(1)} %get-tuple-element.199, ...), kind=kLoop, calls=%fused_computation.17.clone.1 | loop fusion | flops 40857600 | bytes 589824 | tf_op jit(solution)/shard_map/while/body/reduce_sum | solution.py:35
  282.5 0.8 multiply_add_fusion
  (98 shorter events, 16.0 us)
Async XLA Ops:
  7.2 126.8 %all-gather.2.cloned.1.call-start = ((), (), s32[]{:S(2)}) async-start(), calls=%async_computation | async-start | bytes 9732096 | tf_op jit(solution)/shard_map/all_gather | solution.py:69
  7.9 9.9 %collective-permute-start = (f32[3,6,64]{2,1,0:T(8,128)S(1)}, f32[3,6,64]{2,1,0:T(8,128)S(1)}, u32[]{:S(2)}, u32[]{:S(2)}) collective-permute-start(f32[3,6,64]{2,1,0:T(8,128)S(1)} %slice.136), channel_id=1, source_target_pairs={{1,0},{2,1},{3,2},{4,3},{5,4},{6,5},{7,6},{8,7},{9,8},{10,9},{11,1... | collective-permute-start | bytes 13832 | tf_op jit(solution)/shard_map/ppermute | solution.py:18
  133.9 18.3 %copy-start.3 = (s32[1,1,96]{2,1,0:T(1,128)S(1)}, s32[1,1,96]{2,1,0:T(1,128)}, u32[]{:S(2)}) copy-start(s32[1,1,96]{2,1,0:T(1,128)} %param.15) | copy-start | bytes 1156
  152.2 130.3 %copy-start = (f32[3,6,2048]{2,1,0:T(8,128)S(1)}, f32[3,6,2048]{2,1,0:T(8,128)}, u32[]{:S(2)}) copy-start(f32[3,6,2048]{2,1,0:T(8,128)} %param.11) | copy-start | bytes 442372
  152.2 130.3 %copy-start.2 = (f32[3]{0:T(128)S(1)}, f32[3]{0:T(128)}, u32[]{:S(2)}) copy-start(f32[3]{0:T(128)} %constant.91.clone) | copy-start | bytes 40
  282.5 0.8 copy-start.1
Sparse Core Ops, SparseCore 0:
  19.8 78.8 all-gather.1
where the time goes:
time: 291 us; the launch traced here: 290 us
  other arithmetic  177 us (61%)
  blocking collectives  45.8 us (16%)
  local copies, waits for them, and re-layouts  37.7 us (13%)
  between operations  14.3 us (5%)
  waiting for transfers between devices  6.94 us (2%)
  loops' own time  6.44 us (2%)
    reduce_sum x10, other arithmetic, induce(): jnp.sum(cross_x * weight, axis=2)  164 us
    all_gather x1, blocking collectives, body(): all_lists = lax.all_gather(send_lists, 'turb', axis=0, tiled=True)  45.8 us
    all_gather x1, local copies, waits for them, and re-layouts, body(): everyone = lax.all_gather(sources, 'turb', axis=0, tiled=True)  12.7 us
    ppermute x1, waiting for transfers between devices, passed_along(): lax.ppermute(value, axis, [(source, source + steps) for source in range(l...  6.9 us
    another operation x1, loops' own time, body(): total = lax.fori_loop(0, jnp.max(counts), far_step, total)  6.44 us
  transfers between devices with their start and end apart: 2, of which 1 were waited for; matrix products, arithmetic and copies ran while one was open for 24% of the time, Pallas kernels for 0%

commit v1 on v0

v1 whole, which is shorter than its diff:
```python
import functools

import jax
import jax.numpy as jnp
from jax import lax
from jax.experimental import pallas as pl
from jax.experimental.pallas import tpu as pltpu
from jax.sharding import PartitionSpec as P

SPAN = 64
TILE = 128
time_step = 0.1
core_square = 0.25
inflow_speed = 1.0
inv_four_pi = 0.07957747154594767
GROUP = 8
DEPTH = 32
F32 = jnp.float32
BF16 = jnp.bfloat16


def split3(value):
    first = value.astype(BF16).astype(F32)
    rest = value - first
    second = rest.astype(BF16).astype(F32)
    third = (rest - second).astype(BF16).astype(F32)
    return first, second, third


def lattice(pos_ref, circ_ref, next_ref, last_ref):
    ends = last_ref[0] == 1
    middles, strengths = [], []
    for comp in range(3):
        here = pos_ref[comp]
        beyond = jnp.where(ends, here[:, -SPAN:], next_ref[comp])
        segment = jnp.concatenate([here[:, SPAN:], beyond], axis=1) - here
        middles.append(here + 0.5 * segment)
        strengths.append(circ_ref[...] * segment)
    return middles, strengths


def source_rows(middle, strength):
    near_rows = []
    for comp in range(3):
        m1, m2, m3 = split3(-2.0 * middle[comp])
        near_rows += [m1, m2, m1, m2, m3, m1]
    square = middle[0] * middle[0] + middle[1] * middle[1] + middle[2] * middle[2] + core_square
    near_rows += [jnp.ones_like(square)] * 3 + list(split3(square))
    w = [inv_four_pi * s for s in strength]
    u = [
        w[1] * middle[2] - w[2] * middle[1],
        w[2] * middle[0] - w[0] * middle[2],
        w[0] * middle[1] - w[1] * middle[0],
    ]
    parts = [split3(v) for v in w + u]
    strength_rows = []
    for half in (parts[:3], parts[3:]):
        for level in range(3):
            strength_rows += [half[comp][level] for comp in range(3)]
    return near_rows, strength_rows


def target_rows(point):
    rows = []
    for comp in range(3):
        x1, x2, x3 = split3(point[comp])
        rows += [x1, x1, x2, x2, x1, x3]
    square = point[0] * point[0] + point[1] * point[1] + point[2] * point[2]
    rows += list(split3(square)) + [jnp.ones_like(square)] * 3
    return rows


def send_kernel(rows, halves, peers, cap, pos_ref, circ_ref, next_ref, last_ref, list_ref, out_ref, stage):
    middles, strengths = lattice(pos_ref, circ_ref, next_ref, last_ref)
    for comp, field in enumerate(middles + strengths):
        for half in range(halves):
            stage[pl.ds(half * 8 + comp, rows, halves * 8), :] = field[:, half * TILE : (half + 1) * TILE]

    def fill(peer, _):
        for c in range(cap):
            block = list_ref[peer * cap + c]
            data = stage[pl.ds(pl.multiple_of(block * 8, 8), 8), :]
            out_ref[peer, c * 6 : c * 6 + 6, :] = data[:6]
        return 0

    lax.fori_loop(0, peers, fill, 0)


def interact(count, item, tt, ss, ww, acc, dsc, ksc):
    def distances(step):
        for u in range(GROUP):
            target, source = item(step * GROUP + u)
            dsc[u] = lax.dot_general(
                tt[jnp.minimum(target, tt.shape[0] - 1)], ss[source], (((1,), (0,)), ((), ())), preferred_element_type=F32
            )

    def kernels():
        for u in range(GROUP):
            inverse = lax.rsqrt(dsc[u])
            weight = inverse * inverse * inverse
            high = weight.astype(BF16)
            ksc[u, :, :TILE] = high
            ksc[u, :, TILE:] = (weight - high.astype(F32)).astype(BF16)

    def gather(step):
        for u in range(0, GROUP, 2):
            t0, s0 = item(step * GROUP + u)
            t1, s1 = item(step * GROUP + u + 1)
            left = jnp.concatenate([ww[s0], ww[s1]], axis=0)
            left = jnp.concatenate([left, left], axis=1)
            right = ksc[u : u + 2].reshape(2 * TILE, 2 * TILE)
            both = lax.dot_general(left, right, (((1,), (1,)), ((), ())), preferred_element_type=F32)
            r0 = pl.ds(pl.multiple_of(t0 * DEPTH, DEPTH), DEPTH)
            acc[r0, :] = acc[r0, :] + both[:DEPTH, :TILE]
            r1 = pl.ds(pl.multiple_of(t1 * DEPTH, DEPTH), DEPTH)
            acc[r1, :] = acc[r1, :] + both[DEPTH:, TILE:]

    acc[...] = jnp.zeros_like(acc)
    distances(0)
    kernels()
    distances(1)

    def step(index, _):
        gather(index)
        kernels()
        distances(index + 2)
        return 0

    lax.fori_loop(0, count, step, 0)


def near_kernel(
    rows, halves, near, kmax,
    pos_ref, circ_ref, next_ref, last_ref, near_ref, slot_ref, count_ref,
    tt_ref, acc_ref, item_ref, total_ref,
    ss, ww, stage, dsc, ksc,
):
    tiles = rows * halves
    middles, strengths = lattice(pos_ref, circ_ref, next_ref, last_ref)
    points = [pos_ref[comp] for comp in range(3)]

    def lay(fields, start):
        for half in range(halves):
            cut = slice(half * TILE, (half + 1) * TILE)
            for r, field in enumerate(fields):
                stage[pl.ds(half * DEPTH + start + r, rows, halves * DEPTH), :] = field[:, cut]

    stage[...] = jnp.zeros_like(stage)
    near_rows, strength_rows = source_rows(middles, strengths)

    def pack_to(dest):
        def pack(b, _):
            dest[b] = stage[pl.ds(pl.multiple_of(b * DEPTH, DEPTH), DEPTH), :].astype(BF16)
            return 0

        lax.fori_loop(0, tiles, pack, 0, unroll=4)

    lay(near_rows, 0)
    pack_to(ss)
    lay(target_rows(points), 0)

    def turn(b, _):
        tt_ref[b] = stage[pl.ds(pl.multiple_of(b * DEPTH, DEPTH), DEPTH), :].T.astype(BF16)
        return 0

    lax.fori_loop(0, tiles, turn, 0, unroll=4)
    stage[...] = jnp.zeros_like(stage)
    lay(strength_rows, 0)
    pack_to(ww)

    def listed(b, at):
        for k in range(kmax):
            item_ref[at + k] = b * 256 + slot_ref[b * kmax + k]
        return at + count_ref[b]

    total = lax.fori_loop(0, tiles, listed, 0)
    for k in range(3 * GROUP):
        item_ref[total + k] = tiles * 256
    total_ref[0] = total

    last = tiles * near - 1

    def item(i):
        i = jnp.minimum(i, last)
        return i // near, near_ref[i]

    interact(tiles * near // GROUP, item, tt_ref, ss, ww, acc_ref, dsc, ksc)


def far_kernel(
    rows, halves, peers, cap, width_rows,
    pos_ref, recv_ref, tt_ref, near_acc, item_ref, total_ref,
    vel_ref, moved_ref,
    ss, ww, stage, acc, dsc, ksc,
):
    stage[...] = jnp.zeros_like(stage)

    def lay(group, _):
        for c in range(cap):
            parts = [
                recv_ref[pl.ds(group * (8 * width_rows) + c * 6 + comp, 8, width_rows), :] for comp in range(6)
            ]
            near_rows, strength_rows = source_rows(parts[:3], parts[3:])
            for r, field in enumerate(near_rows):
                stage[pl.ds(group * (8 * cap * 64) + c * 64 + r, 8, cap * 64), :] = field
            for r, field in enumerate(strength_rows):
                stage[pl.ds(group * (8 * cap * 64) + c * 64 + 32 + r, 8, cap * 64), :] = field
        return 0

    lax.fori_loop(0, peers // 8, lay, 0)

    def pack(b, _):
        ss[b] = stage[pl.ds(pl.multiple_of(b * 64, 64), 32), :].astype(BF16)
        ww[b] = stage[pl.ds(pl.multiple_of(b * 64 + 32, 32), 32), :].astype(BF16)
        return 0

    lax.fori_loop(0, peers * cap, pack, 0, unroll=4)

    def item(i):
        code = item_ref[i]
        return code // 256, code % 256

    total = total_ref[0]
    interact((total + GROUP - 1) // GROUP, item, tt_ref, ss, ww, acc, dsc, ksc)

    for half in range(halves):
        cut = slice(half * TILE, (half + 1) * TILE)
        sums = []
        for first in (0, 9):
            for comp in range(3):
                value = None
                for level in (2, 1, 0):
                    where = pl.ds(half * DEPTH + first + level * 3 + comp, rows, halves * DEPTH)
                    term = acc[where, :] + near_acc[where, :]
                    value = term if value is None else value + term
                sums.append(value)
        point = [pos_ref[comp, :, cut] for comp in range(3)]
        for comp in range(3):
            j, k = (comp + 1) % 3, (comp + 2) % 3
            velocity = sums[j] * point[k] - sums[k] * point[j] - sums[3 + comp]
            vel_ref[comp, :, cut] = velocity
            inflow = inflow_speed if comp == 0 else 0.0
            moved_ref[comp, :, cut] = point[comp] + time_step * (velocity + inflow)


def body(positions, circulation, send_lists, reader_slots, source_counts, near_blocks):
    _, rows, width = positions.shape
    halves = width // TILE
    tiles = rows * halves
    peers = lax.axis_size("turb")
    cap = send_lists.shape[-1]
    kmax = reader_slots.shape[-1]
    near = near_blocks.shape[-1]
    vmem = pl.BlockSpec(memory_space=pltpu.VMEM)
    smem = pl.BlockSpec(memory_space=pltpu.SMEM)
    ages = lax.axis_size("age")
    next_row = lax.ppermute(positions[:, :, :SPAN], "age", [(s, s - 1) for s in range(1, ages)])
    last = (lax.axis_index("age") == ages - 1).astype(jnp.int32).reshape(1)
    width_rows = -(-cap * 6 // 8) * 8
    params = pltpu.CompilerParams(vmem_limit_bytes=48 << 20)

    outgoing = pl.pallas_call(
        functools.partial(send_kernel, rows, halves, peers, cap),
        out_shape=jax.ShapeDtypeStruct((peers, width_rows, TILE), F32),
        in_specs=[vmem, vmem, vmem, smem, smem],
        out_specs=vmem,
        scratch_shapes=[pltpu.VMEM((tiles * 8, TILE), F32)],
        compiler_params=params,
    )(positions, circulation, next_row, last, send_lists.reshape(-1))
    incoming = lax.all_to_all(outgoing, "turb", 0, 0, tiled=True).reshape(peers * width_rows, TILE)

    pairs = [pltpu.VMEM((GROUP, TILE, TILE), F32), pltpu.VMEM((GROUP, TILE, 2 * TILE), BF16)]
    turned, near_acc, items, total = pl.pallas_call(
        functools.partial(near_kernel, rows, halves, near, kmax),
        out_shape=(
            jax.ShapeDtypeStruct((tiles, TILE, DEPTH), BF16),
            jax.ShapeDtypeStruct((tiles * DEPTH, TILE), F32),
            jax.ShapeDtypeStruct((tiles * kmax + 4 * GROUP,), jnp.int32),
            jax.ShapeDtypeStruct((1,), jnp.int32),
        ),
        in_specs=[vmem, vmem, vmem, smem, smem, smem, smem],
        out_specs=(vmem, vmem, smem, smem),
        scratch_shapes=[
            pltpu.VMEM((tiles, DEPTH, TILE), BF16),
            pltpu.VMEM((tiles, DEPTH, TILE), BF16),
            pltpu.VMEM((tiles * DEPTH, TILE), F32),
            *pairs,
        ],
        compiler_params=params,
        cost_estimate=pl.CostEstimate(flops=2 * 10**9, bytes_accessed=4 << 20, transcendentals=tiles * near * TILE * TILE),
    )(
        positions, circulation, next_row, last,
        near_blocks.reshape(-1), reader_slots.reshape(-1), source_counts.reshape(-1),
    )
    return pl.pallas_call(
        functools.partial(far_kernel, rows, halves, peers, cap, width_rows),
        out_shape=(
            jax.ShapeDtypeStruct(positions.shape, F32),
            jax.ShapeDtypeStruct(positions.shape, F32),
        ),
        in_specs=[vmem, vmem, vmem, vmem, smem, smem],
        out_specs=(vmem, vmem),
        scratch_shapes=[
            pltpu.VMEM((peers * cap, DEPTH, TILE), BF16),
            pltpu.VMEM((peers * cap, DEPTH, TILE), BF16),
            pltpu.VMEM((peers * cap * 64, TILE), F32),
            pltpu.VMEM(((tiles + 1) * DEPTH, TILE), F32),
            *pairs,
        ],
        compiler_params=params,
    )(positions, incoming, turned, near_acc, items, total)


def solution(mesh):
    in_specs = (
        P(None, "turb", "age"),
        P("turb", "age"),
        P("turb", "age", None, None),
        P("turb", "age", None, None),
        P("turb", "age", None),
        P("turb", "age", None, None),
    )
    out_specs = (P(None, "turb", "age"), P(None, "turb", "age"))
    return jax.shard_map(body, mesh=mesh, in_specs=in_specs, out_specs=out_specs, check_vma=False)
```

time: 291 us -> 90.7 us (0.31)
  the two profiles are of different devices: /device:TPU:131 before, /device:TPU:29 now
where the time goes in v1:
time: 90.7 us; the launch traced here: 90.2 us
  Pallas kernels  59.6 us (66%)
  starting transfers between devices  19.8 us (22%)
  local copies, waits for them, and re-layouts  10.1 us (11%)
    pallas_call x1, Pallas kernels, body(): pl.pallas_call(functools.partial(far_kernel, rows, halves, peers, cap, wi...  30.3 us
    pallas_call x1, Pallas kernels, body(): pl.pallas_call(functools.partial(near_kernel, rows, halves, near, kmax),...  27.3 us
    ppermute x1, starting transfers between devices, body(): lax.ppermute(positions[:, :, :SPAN], 'age', [(s, s - 1) for s in range(1,...  12.4 us
    unnamed x19, local copies, waits for them, and re-layouts  9.07 us
    all_to_all x1, starting transfers between devices, body(): lax.all_to_all(outgoing, 'turb', 0, 0, tiled=True)  7.39 us
    pallas_call x1, Pallas kernels, body(): pl.pallas_call(functools.partial(send_kernel, rows, halves, peers, cap),...  1.97 us
  transfers between devices with their start and end apart: 2, of which 0 were waited for; matrix products, arithmetic and copies ran while one was open for 3% of the time, Pallas kernels for 30%

profile of v1, /device:TPU:29, one launch (start us, length us, event | category | flops | bytes accessed | tf_op | source)
XLA Modules:
  0.0 90.2 jit_solution(2023560801445542329)
XLA Ops:
  0.6 0.7 slice.3
  1.3 12.4 %collective-permute-start = (f32[3,6,64]{2,1,0:T(8,128)S(1)}, f32[3,6,64]{2,1,0:T(8,128)S(1)}, u32[]{:S(2)}, u32[]{:S(2)}) collective-permute-start(f32[3,6,64]{2,1,0:T(8,128)S(1)} %slice.3), channel_id=1, source_target_pairs={{1,0},{2,1},{3,2},{4,3},{5,4},{6,5},{7,6},{8,7},{9,8},{10,9},{11,1... | collective-permute-start | bytes 13832 | tf_op jit(solution)/shard_map/ppermute | solution.py:257
  13.8 0.8 copy.8
  14.5 0.1 reshape.26.list_ref
  14.6 0.0 collective-permute-done.next_ref
  14.7 0.0 copy-start.2
  14.7 0.9 %copy-done.2 = f32[3,6,2048]{2,1,0:T(8,128)S(1)} copy-done((f32[3,6,2048]{2,1,0:T(8,128)S(1)}, f32[3,6,2048]{2,1,0:T(8,128)}, u32[]{:S(2)}) %copy-start.2) | copy-done | bytes 147480
  15.6 0.0 copy-start.5
  15.6 0.8 copy-done.5
  16.4 2.0 %shard_map.77 = f32[32,40,128]{2,1,0:T(8,128)} custom-call(f32[3,6,2048]{2,1,0:T(8,128)S(1)} %copy-done.2, f32[6,2048]{1,0:T(8,128)S(1)} %copy-done.5, f32[3,6,64]{2,1,0:T(8,128)S(1)} %collective-permute-done.next_ref, s32[1]{0:T(128)} %bitcast.last_ref, s32[192]{0:T(256)S(1)} %reshape.26.list_ref), custom_call_target="tpu_custom_call" | custom-call | tf_op jit(solution)/shard_map/pallas_call | solution.py:262
  18.4 7.4 %all-to-all-start = ((f32[32,40,128]{2,1,0:T(8,128)}), f32[32,40,128]{2,1,0:T(8,128)}, u32[]{:S(2)}, u32[]{:S(2)}) async-start(f32[32,40,128]{2,1,0:T(8,128)} %shard_map.77), calls=%async_computation | async-start | bytes 1310720 | tf_op jit(solution)/shard_map/all_to_all | solution.py:270
  25.8 0.8 copy.10
  26.6 0.1 reshape.29.slot_ref
  26.7 0.8 copy.9
  27.4 0.1 reshape.28.near_ref
  27.6 0.0 copy-start.3
  27.6 0.9 %copy-done.3 = f32[3,6,2048]{2,1,0:T(8,128)S(1)} copy-done((f32[3,6,2048]{2,1,0:T(8,128)S(1)}, f32[3,6,2048]{2,1,0:T(8,128)}, u32[]{:S(2)}) %copy-start.3) | copy-done | bytes 147480
  28.5 0.0 copy-start.6
  28.5 0.8 copy-done.6
  29.3 0.0 copy-start.7
  29.3 0.7 copy-done.7
  30.0 0.0 copy-start.4
  30.0 27.3 %shard_map.78 = (bf16[96,128,32]{2,1,0:T(8,128)(2,1)S(1)}, f32[3072,128]{1,0:T(8,128)S(1)}, s32[800]{0:T(1024)S(1)}, s32[1]{0:T(128)}) custom-call(f32[3,6,2048]{2,1,0:T(8,128)S(1)} %copy-done.3, f32[6,2048]{1,0:T(8,128)S(1)} %copy-done.6, f32[3,6,64]{2,1,0:T(8,128)S(1)} %collective-permute-done.next_ref, s32[1]{0:T(128)} %bitcast.last_ref, ...), custom_call_target="tpu_custom_call" | custom-call | flops 2000000000 | bytes 4194304 | tf_op jit(solution)/shard_map/pallas_call | solution.py:273
  57.3 0.0 copy-start
  57.3 1.1 %copy-done = f32[3072,128]{1,0:T(8,128)} copy-done((f32[3072,128]{1,0:T(8,128)}, f32[3072,128]{1,0:T(8,128)S(1)}, u32[]{:S(2)}) %copy-start) | copy-done | bytes 1572888
  58.4 0.0 all-to-all-done
  58.4 0.0 copy-done.4
  58.4 0.0 copy-start.1
  58.4 1.4 %copy-done.1 = f32[3072,128]{1,0:T(8,128)S(1)} copy-done((f32[3072,128]{1,0:T(8,128)S(1)}, f32[3072,128]{1,0:T(8,128)}, u32[]{:S(2)}) %copy-start.1) | copy-done | bytes 1572888
  59.8 30.3 %shard_map.79 = (f32[3,6,2048]{2,1,0:T(8,128)}, f32[3,6,2048]{2,1,0:T(8,128)}) custom-call(f32[3,6,2048]{2,1,0:T(8,128)S(1)} %copy-done.4, f32[1280,128]{1,0:T(8,128)} %bitcast.1.recv_ref, bf16[96,128,32]{2,1,0:T(8,128)(2,1)S(1)} %get-tuple-element.6.tt_ref, f32[3072,128]{1,0:T(8,128)S(1)} %copy-done.1, s32[800]{0:T(1024)S(1)} %get-tuple-element.8.item_ref, ...), custom_call_target="tpu_custom_call" | custom-call | tf_op jit(solution)/shard_map/pallas_call | solution.py:295
Async XLA Ops:
  1.3 13.3 %collective-permute-start = (f32[3,6,64]{2,1,0:T(8,128)S(1)}, f32[3,6,64]{2,1,0:T(8,128)S(1)}, u32[]{:S(2)}, u32[]{:S(2)}) collective-permute-start(f32[3,6,64]{2,1,0:T(8,128)S(1)} %slice.3), channel_id=1, source_target_pairs={{1,0},{2,1},{3,2},{4,3},{5,4},{6,5},{7,6},{8,7},{9,8},{10,9},{11,1... | collective-permute-start | bytes 13832 | tf_op jit(solution)/shard_map/ppermute | solution.py:257
  14.7 0.9 %copy-start.2 = (f32[3,6,2048]{2,1,0:T(8,128)S(1)}, f32[3,6,2048]{2,1,0:T(8,128)}, u32[]{:S(2)}) copy-start(f32[3,6,2048]{2,1,0:T(8,128)} %pos_ref.5) | copy-start | bytes 442372
  15.6 0.8 copy-start.5
  18.4 40.0 %all-to-all-start = ((f32[32,40,128]{2,1,0:T(8,128)}), f32[32,40,128]{2,1,0:T(8,128)}, u32[]{:S(2)}, u32[]{:S(2)}) async-start(f32[32,40,128]{2,1,0:T(8,128)} %shard_map.77), calls=%async_computation | async-start | bytes 1310720 | tf_op jit(solution)/shard_map/all_to_all | solution.py:270
  27.6 0.9 %copy-start.3 = (f32[3,6,2048]{2,1,0:T(8,128)S(1)}, f32[3,6,2048]{2,1,0:T(8,128)}, u32[]{:S(2)}) copy-start(f32[3,6,2048]{2,1,0:T(8,128)} %pos_ref.5) | copy-start | bytes 442372
  28.5 0.8 copy-start.6
  29.3 0.7 copy-start.7
  30.0 28.5 %copy-start.4 = (f32[3,6,2048]{2,1,0:T(8,128)S(1)}, f32[3,6,2048]{2,1,0:T(8,128)}, u32[]{:S(2)}) copy-start(f32[3,6,2048]{2,1,0:T(8,128)} %pos_ref.5) | copy-start | bytes 442372
  57.3 1.2 %copy-start = (f32[3072,128]{1,0:T(8,128)}, f32[3072,128]{1,0:T(8,128)S(1)}, u32[]{:S(2)}) copy-start(f32[3072,128]{1,0:T(8,128)S(1)} %get-tuple-element.7.near_acc) | copy-start | bytes 4718596
  58.4 1.4 %copy-start.1 = (f32[3072,128]{1,0:T(8,128)S(1)}, f32[3072,128]{1,0:T(8,128)}, u32[]{:S(2)}) copy-start(f32[3072,128]{1,0:T(8,128)} %copy-done) | copy-start | bytes 4718596

commit v2 on v1

v2 whole, which is shorter than its diff:
```python
import functools

import jax
import jax.numpy as jnp
from jax import lax
from jax.experimental import pallas as pl
from jax.experimental.pallas import tpu as pltpu
from jax.sharding import PartitionSpec as P

SPAN = 64
TILE = 128
time_step = 0.1
core_square = 0.25
inflow_speed = 1.0
inv_four_pi = 0.07957747154594767
GROUP = 8
STEPS = 4
DEPTH = 32
SUMS = 16
F32 = jnp.float32
BF16 = jnp.bfloat16


def split3(value):
    first = value.astype(BF16).astype(F32)
    rest = value - first
    second = rest.astype(BF16).astype(F32)
    third = (rest - second).astype(BF16).astype(F32)
    return first, second, third


def lattice(pos_ref, circ_ref, next_ref, last_ref):
    ends = last_ref[0] == 1
    middles, strengths = [], []
    for comp in range(3):
        here = pos_ref[comp]
        beyond = jnp.where(ends, here[:, -SPAN:], next_ref[comp])
        segment = jnp.concatenate([here[:, SPAN:], beyond], axis=1) - here
        middles.append(here + 0.5 * segment)
        strengths.append(circ_ref[...] * segment)
    return middles, strengths


def source_rows(middle, strength):
    near_rows = []
    for comp in range(3):
        m1, m2, m3 = split3(-2.0 * middle[comp])
        near_rows += [m1, m2, m1, m2, m3, m1]
    square = middle[0] * middle[0] + middle[1] * middle[1] + middle[2] * middle[2] + core_square
    zero = jnp.zeros_like(square)
    near_rows += [jnp.ones_like(square)] * 3 + list(split3(square)) + [zero] * 8
    w1, w2, w = [], [], []
    for comp in range(3):
        first, second, _ = split3(inv_four_pi * strength[comp])
        w1.append(first)
        w2.append(second)
        w.append(first + second)
    u = [
        split3(w[1] * middle[2] - w[2] * middle[1]),
        split3(w[2] * middle[0] - w[0] * middle[2]),
        split3(w[0] * middle[1] - w[1] * middle[0]),
    ]
    strength_rows = w1 + w2 + [u[comp][level] for level in range(3) for comp in range(3)] + [zero]
    return near_rows, strength_rows


def target_rows(point):
    rows = []
    for comp in range(3):
        x1, x2, x3 = split3(point[comp])
        rows += [x1, x1, x2, x2, x1, x3]
    square = point[0] * point[0] + point[1] * point[1] + point[2] * point[2]
    rows += list(split3(square)) + [jnp.ones_like(square)] * 3 + [jnp.zeros_like(square)] * 8
    return rows


def send_kernel(rows, halves, peers, cap, pos_ref, circ_ref, next_ref, last_ref, list_ref, out_ref, stage):
    middles, strengths = lattice(pos_ref, circ_ref, next_ref, last_ref)
    for comp, field in enumerate(middles + strengths):
        for half in range(halves):
            stage[pl.ds(half * 8 + comp, rows, halves * 8), :] = field[:, half * TILE : (half + 1) * TILE]

    def fill(peer, _):
        for c in range(cap):
            block = list_ref[c, 0, peer]
            data = stage[pl.ds(pl.multiple_of(block * 8, 8), 8), :]
            out_ref[peer, c * 6 : c * 6 + 6, :] = data[:6]
        return 0

    lax.fori_loop(0, peers, fill, 0)


def interact(count, item, tt, st, ww, acc, dsc, ksc):
    most = tt.shape[0] - 1

    def distances(step, side):
        for u in range(GROUP):
            target, source = item(step * GROUP + u)
            half = slice((u % 2) * TILE, (u % 2 + 1) * TILE)
            dsc[side, u // 2, :, half] = lax.dot_general(
                st[source], tt[jnp.minimum(target, most)], (((1,), (0,)), ((), ())), preferred_element_type=F32
            )

    def kernels(side):
        for u in range(GROUP // 2):
            inverse = lax.rsqrt(dsc[side, u])
            weight = inverse * inverse * inverse
            high = weight.astype(BF16)
            ksc[side, u, :TILE] = high
            ksc[side, u, TILE:] = (weight - high.astype(F32)).astype(BF16)

    def gather(step, side):
        for u in range(0, GROUP, 2):
            t0, s0 = item(step * GROUP + u)
            t1, s1 = item(step * GROUP + u + 1)
            left = jnp.concatenate([ww[s0], ww[s1]], axis=0)
            left = jnp.concatenate([left, left], axis=1)
            both = lax.dot_general(left, ksc[side, u // 2], (((1,), (0,)), ((), ())), preferred_element_type=F32)
            r0 = pl.ds(pl.multiple_of(t0 * SUMS, SUMS), SUMS)
            acc[r0, :] = acc[r0, :] + both[:SUMS, :TILE]
            r1 = pl.ds(pl.multiple_of(t1 * SUMS, SUMS), SUMS)
            acc[r1, :] = acc[r1, :] + both[SUMS:, TILE:]

    distances(0, 0)
    kernels(0)
    distances(1, 1)

    def turn(index, _):
        for h in range(STEPS):
            step, side = index * STEPS + h, h % 2
            gather(step, side)
            kernels(1 - side)
            distances(step + 2, side)
        return 0

    lax.fori_loop(0, count, turn, 0)


def near_kernel(
    rows, halves, near, kmax,
    pos_ref, circ_ref, next_ref, last_ref, near_ref, slot_ref, count_ref,
    tt_ref, acc_ref, item_ref, total_ref,
    st, ww, stage, dsc, ksc,
):
    tiles = rows * halves
    middles, strengths = lattice(pos_ref, circ_ref, next_ref, last_ref)
    points = [pos_ref[comp] for comp in range(3)]
    deep = 2 * DEPTH + SUMS

    def lay(fields, start):
        for half in range(halves):
            cut = slice(half * TILE, (half + 1) * TILE)
            for r, field in enumerate(fields):
                stage[pl.ds(half * deep + start + r, rows, halves * deep), :] = field[:, cut]

    near_rows, strength_rows = source_rows(middles, strengths)
    lay(near_rows + target_rows(points) + strength_rows, 0)

    def pack(b, _):
        base = pl.multiple_of(b * deep, SUMS)
        st[b] = stage[pl.ds(base, DEPTH), :].T.astype(BF16)
        tt_ref[b] = stage[pl.ds(base + DEPTH, DEPTH), :].astype(BF16)
        ww[b] = stage[pl.ds(base + 2 * DEPTH, SUMS), :].astype(BF16)
        return 0

    lax.fori_loop(0, tiles, pack, 0, unroll=8)

    def listed(b, at):
        for k in range(kmax):
            item_ref[at + k] = b * 256 + slot_ref[k, b]
        return at + count_ref[b]

    total = lax.fori_loop(0, tiles, listed, 0)
    for k in range((STEPS + 2) * GROUP):
        item_ref[total + k] = tiles * 256
    total_ref[0] = total

    last = tiles * near - 1

    def item(i):
        i = jnp.minimum(i, last)
        b = lax.div(i, near)
        return b, near_ref[i - b * near, b]

    acc_ref[...] = jnp.zeros_like(acc_ref)
    interact(tiles * near // (STEPS * GROUP), item, tt_ref, st, ww, acc_ref, dsc, ksc)


def far_kernel(
    rows, halves, peers, cap, width_rows,
    pos_ref, recv_ref, tt_ref, near_acc, item_ref, total_ref,
    vel_ref, moved_ref,
    st, ww, stage, acc, dsc, ksc,
):
    deep = DEPTH + SUMS

    def lay(group, _):
        for c in range(cap):
            parts = [
                recv_ref[pl.ds(group * (8 * width_rows) + c * 6 + comp, 8, width_rows), :] for comp in range(6)
            ]
            near_rows, strength_rows = source_rows(parts[:3], parts[3:])
            for r, field in enumerate(near_rows + strength_rows):
                stage[pl.ds(group * (8 * cap * deep) + c * deep + r, 8, cap * deep), :] = field
        return 0

    lax.fori_loop(0, peers // 8, lay, 0)

    def pack(b, _):
        base = pl.multiple_of(b * deep, SUMS)
        st[b] = stage[pl.ds(base, DEPTH), :].T.astype(BF16)
        ww[b] = stage[pl.ds(base + DEPTH, SUMS), :].astype(BF16)
        return 0

    lax.fori_loop(0, peers * cap, pack, 0, unroll=8)

    def item(i):
        code = item_ref[i]
        return lax.shift_right_logical(code, 8), lax.bitwise_and(code, 255)

    acc[: rows * halves * SUMS, :] = near_acc[...]
    turns = lax.div(total_ref[0] + STEPS * GROUP - 1, STEPS * GROUP)
    interact(turns, item, tt_ref, st, ww, acc, dsc, ksc)

    for half in range(halves):
        cut = slice(half * TILE, (half + 1) * TILE)

        def summed(*lines):
            value = None
            for line in lines:
                term = acc[pl.ds(half * SUMS + line, rows, halves * SUMS), :]
                value = term if value is None else value + term
            return value

        sums = [summed(3 + comp, comp) for comp in range(3)]
        cross = [summed(12 + comp, 9 + comp, 6 + comp) for comp in range(3)]
        point = [pos_ref[comp, :, cut] for comp in range(3)]
        for comp in range(3):
            j, k = (comp + 1) % 3, (comp + 2) % 3
            velocity = sums[j] * point[k] - sums[k] * point[j] - cross[comp]
            vel_ref[comp, :, cut] = velocity
            inflow = inflow_speed if comp == 0 else 0.0
            moved_ref[comp, :, cut] = point[comp] + time_step * (velocity + inflow)


def body(positions, circulation, send_lists, reader_slots, source_counts, near_blocks):
    _, rows, width = positions.shape
    halves = width // TILE
    tiles = rows * halves
    peers = lax.axis_size("turb")
    cap = send_lists.shape[-1]
    kmax = reader_slots.shape[-1]
    near = near_blocks.shape[-1]
    vmem = pl.BlockSpec(memory_space=pltpu.VMEM)
    smem = pl.BlockSpec(memory_space=pltpu.SMEM)
    ages = lax.axis_size("age")
    next_row = lax.ppermute(positions[:, :, :SPAN], "age", [(s, s - 1) for s in range(1, ages)])
    last = (lax.axis_index("age") == ages - 1).astype(jnp.int32).reshape(1)
    width_rows = -(-cap * 6 // 8) * 8
    params = pltpu.CompilerParams(vmem_limit_bytes=48 << 20)

    outgoing = pl.pallas_call(
        functools.partial(send_kernel, rows, halves, peers, cap),
        out_shape=jax.ShapeDtypeStruct((peers, width_rows, TILE), F32),
        in_specs=[vmem, vmem, vmem, smem, smem],
        out_specs=vmem,
        scratch_shapes=[pltpu.VMEM((tiles * 8, TILE), F32)],
        compiler_params=params,
    )(positions, circulation, next_row, last, send_lists[0, 0].T[:, None])
    incoming = lax.all_to_all(outgoing, "turb", 0, 0, tiled=True).reshape(peers * width_rows, TILE)

    pairs = [
        pltpu.VMEM((2, GROUP // 2, TILE, 2 * TILE), F32),
        pltpu.VMEM((2, GROUP // 2, 2 * TILE, 2 * TILE), BF16),
    ]
    targets, near_acc, items, total = pl.pallas_call(
        functools.partial(near_kernel, rows, halves, near, kmax),
        out_shape=(
            jax.ShapeDtypeStruct((tiles, DEPTH, TILE), BF16),
            jax.ShapeDtypeStruct((tiles * SUMS, TILE), F32),
            jax.ShapeDtypeStruct((tiles * kmax + 64,), jnp.int32),
            jax.ShapeDtypeStruct((1,), jnp.int32),
        ),
        in_specs=[vmem, vmem, vmem, smem, smem, smem, smem],
        out_specs=(vmem, vmem, smem, smem),
        scratch_shapes=[
            pltpu.VMEM((tiles, TILE, DEPTH), BF16),
            pltpu.VMEM((tiles, SUMS, TILE), BF16),
            pltpu.VMEM((tiles * (2 * DEPTH + SUMS), TILE), F32),
            *pairs,
        ],
        compiler_params=params,
        cost_estimate=pl.CostEstimate(flops=2 * 10**9, bytes_accessed=4 << 20, transcendentals=tiles * near * TILE * TILE),
    )(positions, circulation, next_row, last, near_blocks[0, 0].T, reader_slots[0, 0].T, source_counts[0, 0])
    return pl.pallas_call(
        functools.partial(far_kernel, rows, halves, peers, cap, width_rows),
        out_shape=(
            jax.ShapeDtypeStruct(positions.shape, F32),
            jax.ShapeDtypeStruct(positions.shape, F32),
        ),
        in_specs=[vmem, vmem, vmem, vmem, smem, smem],
        out_specs=(vmem, vmem),
        scratch_shapes=[
            pltpu.VMEM((peers * cap, TILE, DEPTH), BF16),
            pltpu.VMEM((peers * cap, SUMS, TILE), BF16),
            pltpu.VMEM((peers * cap * (DEPTH + SUMS), TILE), F32),
            pltpu.VMEM(((tiles + 1) * SUMS, TILE), F32),
            *pairs,
        ],
        compiler_params=params,
    )(positions, incoming, targets, near_acc, items, total)


def solution(mesh):
    in_specs = (
        P(None, "turb", "age"),
        P("turb", "age"),
        P("turb", "age", None, None),
        P("turb", "age", None, None),
        P("turb", "age", None),
        P("turb", "age", None, None),
    )
    out_specs = (P(None, "turb", "age"), P(None, "turb", "age"))
    return jax.shard_map(body, mesh=mesh, in_specs=in_specs, out_specs=out_specs, check_vma=False)
```

time: 90.7 us -> 68.2 us (0.75)
  the two profiles are of different devices: /device:TPU:29 before, /device:TPU:2 now
where the time goes in v2:
time: 68.2 us; the launch traced here: 67.8 us
  Pallas kernels  42.2 us (62%)
  starting transfers between devices  19.1 us (28%)
  local copies, waits for them, and re-layouts  3.83 us (6%)
  waiting for transfers between devices  1.97 us (3%)
  between operations  0.71 us (1%)
    pallas_call x1, Pallas kernels, body(): pl.pallas_call(functools.partial(far_kernel, rows, halves, peers, cap, wi...  22.6 us
    pallas_call x1, Pallas kernels, body(): pl.pallas_call(functools.partial(near_kernel, rows, halves, near, kmax),...  17.5 us
    ppermute x1, starting transfers between devices, body(): lax.ppermute(positions[:, :, :SPAN], 'age', [(s, s - 1) for s in range(1,...  12.7 us
    all_to_all x1, starting transfers between devices, body(): lax.all_to_all(outgoing, 'turb', 0, 0, tiled=True)  6.36 us
    unnamed x17, local copies, waits for them, and re-layouts  3.1 us
    pallas_call x1, Pallas kernels, body(): pl.pallas_call(functools.partial(send_kernel, rows, halves, peers, cap),...  2.06 us
  transfers between devices with their start and end apart: 2, of which 2 were waited for; matrix products, arithmetic and copies ran while one was open for 0% of the time, Pallas kernels for 26%

profile of v2, /device:TPU:2, one launch (start us, length us, event | category | flops | bytes accessed | tf_op | source)
XLA Modules:
  0.0 67.8 jit_solution(4110162199370821411)
XLA Ops:
  0.6 0.7 %slice.3 = f32[3,6,64]{2,1,0:T(8,128)S(1)} slice(f32[3,6,2048]{2,1,0:T(8,128)} %pos_ref.5), slice={[0:3], [0:6], [0:64]} | slice | bytes 9216 | tf_op jit(solution)/shard_map/slice | solution.py:257
  1.3 12.7 %collective-permute-start = (f32[3,6,64]{2,1,0:T(8,128)S(1)}, f32[3,6,64]{2,1,0:T(8,128)S(1)}, u32[]{:S(2)}, u32[]{:S(2)}) collective-permute-start(f32[3,6,64]{2,1,0:T(8,128)S(1)} %slice.3), channel_id=1, source_target_pairs={{1,0},{2,1},{3,2},{4,3},{5,4},{6,5},{7,6},{8,7},{9,8},{10,9},{11,1... | collective-permute-start | bytes 13832 | tf_op jit(solution)/shard_map/ppermute | solution.py:257
  14.1 0.0 copy-start.7
  14.1 0.7 copy-done.7
  14.8 0.7 %collective-permute-done.next_ref = f32[3,6,64]{2,1,0:T(8,128)S(1)} collective-permute-done((f32[3,6,64]{2,1,0:T(8,128)S(1)}, f32[3,6,64]{2,1,0:T(8,128)S(1)}, u32[]{:S(2)}, u32[]{:S(2)}) %collective-permute-start) | collective-permute-done | bytes 4640 | tf_op jit(solution)/shard_map/ppermute | solution.py:257
  15.4 0.0 copy-start
  15.4 0.9 %copy-done = f32[3,6,2048]{2,1,0:T(8,128)S(1)} copy-done((f32[3,6,2048]{2,1,0:T(8,128)S(1)}, f32[3,6,2048]{2,1,0:T(8,128)}, u32[]{:S(2)}) %copy-start) | copy-done | bytes 147480
  16.4 0.0 copy-start.2
  16.4 0.8 %copy-done.2 = f32[6,2048]{1,0:T(8,128)S(1)} copy-done((f32[6,2048]{1,0:T(8,128)S(1)}, f32[6,2048]{1,0:T(8,128)}, u32[]{:S(2)}) %copy-start.2) | copy-done | bytes 49176
  17.2 2.1 %shard_map.77 = f32[32,40,128]{2,1,0:T(8,128)} custom-call(f32[3,6,2048]{2,1,0:T(8,128)S(1)} %copy-done, f32[6,2048]{1,0:T(8,128)S(1)} %copy-done.2, f32[3,6,64]{2,1,0:T(8,128)S(1)} %collective-permute-done.next_ref, s32[1]{0:T(128)} %bitcast.last_ref, s32[6,1,32]{2,1,0:T(1,128)S(1)} %broadcast_in_dim.3.list_ref), custom_call_target="tpu_custom_call" | custom-call | tf_op jit(solution)/shard_map/pallas_call | solution.py:262
  19.3 0.0 copy-start.1
  19.3 0.0 copy-start.3
  19.3 0.0 copy-start.5
  19.3 6.4 %all-to-all-start = ((f32[32,40,128]{2,1,0:T(8,128)}), f32[32,40,128]{2,1,0:T(8,128)S(1)}, u32[]{:S(2)}, u32[]{:S(2)}) async-start(f32[32,40,128]{2,1,0:T(8,128)} %shard_map.77), calls=%async_computation | async-start | bytes 1310720 | tf_op jit(solution)/shard_map/all_to_all | solution.py:270
  25.6 0.0 copy-start.4
  25.6 0.0 copy-start.6
  25.7 0.0 copy-done.1
  25.7 0.0 copy-done.3
  25.7 0.0 copy-done.5
  25.7 0.6 copy-done.4
  26.3 0.0 copy-done.6
  26.3 17.5 %shard_map.78 = (bf16[96,32,128]{2,1,0:T(8,128)(2,1)S(1)}, f32[1536,128]{1,0:T(8,128)S(1)}, s32[832]{0:T(1024)S(1)}, s32[1]{0:T(128)}) custom-call(f32[3,6,2048]{2,1,0:T(8,128)S(1)} %copy-done.1, f32[6,2048]{1,0:T(8,128)S(1)} %copy-done.3, f32[3,6,64]{2,1,0:T(8,128)S(1)} %collective-permute-done.next_ref, s32[1]{0:T(128)} %bitcast.last_ref, ...), custom_call_target="tpu_custom_call" | custom-call | flops 2000000000 | bytes 4194304 | tf_op jit(solution)/shard_map/pallas_call | solution.py:276
  43.9 1.3 %all-to-all-done = f32[32,40,128]{2,1,0:T(8,128)S(1)} async-done(((f32[32,40,128]{2,1,0:T(8,128)}), f32[32,40,128]{2,1,0:T(8,128)S(1)}, u32[]{:S(2)}, u32[]{:S(2)}) %all-to-all-start) | async-done | bytes 655392 | tf_op jit(solution)/shard_map/all_to_all | solution.py:270
  45.2 22.6 %shard_map.79 = (f32[3,6,2048]{2,1,0:T(8,128)}, f32[3,6,2048]{2,1,0:T(8,128)}) custom-call(f32[3,6,2048]{2,1,0:T(8,128)S(1)} %copy-done.1, f32[1280,128]{1,0:T(8,128)S(1)} %bitcast.14, bf16[96,32,128]{2,1,0:T(8,128)(2,1)S(1)} %get-tuple-element.6.tt_ref, f32[1536,128]{1,0:T(8,128)S(1)} %get-tuple-element.7.near_acc, s32[832]{0:T(1024)S(1)} %get-tuple-element.8.item_ref, ...), custom_call_target="tpu_custom_call" | custom-call | tf_op jit(solution)/shard_map/pallas_call | solution.py:295
  (2 shorter events, 0.0 us)
Async XLA Ops:
  1.3 14.1 %collective-permute-start = (f32[3,6,64]{2,1,0:T(8,128)S(1)}, f32[3,6,64]{2,1,0:T(8,128)S(1)}, u32[]{:S(2)}, u32[]{:S(2)}) collective-permute-start(f32[3,6,64]{2,1,0:T(8,128)S(1)} %slice.3), channel_id=1, source_target_pairs={{1,0},{2,1},{3,2},{4,3},{5,4},{6,5},{7,6},{8,7},{9,8},{10,9},{11,1... | collective-permute-start | bytes 13832 | tf_op jit(solution)/shard_map/ppermute | solution.py:257
  14.1 0.7 %copy-start.7 = (s32[1,1,32,6]{2,1,3,0:T(1,128)S(1)}, s32[1,1,32,6]{2,1,3,0:T(1,128)}, u32[]{:S(2)}) copy-start(s32[1,1,32,6]{2,1,3,0:T(1,128)} %param.8) | copy-start | bytes 2308
  15.4 0.9 %copy-start = (f32[3,6,2048]{2,1,0:T(8,128)S(1)}, f32[3,6,2048]{2,1,0:T(8,128)}, u32[]{:S(2)}) copy-start(f32[3,6,2048]{2,1,0:T(8,128)} %pos_ref.5) | copy-start | bytes 442372
  16.4 0.8 %copy-start.2 = (f32[6,2048]{1,0:T(8,128)S(1)}, f32[6,2048]{1,0:T(8,128)}, u32[]{:S(2)}) copy-start(f32[6,2048]{1,0:T(8,128)} %circ_ref.3) | copy-start | bytes 147460
  19.3 6.4 %copy-start.1 = (f32[3,6,2048]{2,1,0:T(8,128)S(1)}, f32[3,6,2048]{2,1,0:T(8,128)}, u32[]{:S(2)}) copy-start(f32[3,6,2048]{2,1,0:T(8,128)} %pos_ref.5) | copy-start | bytes 442372
  19.3 6.4 %copy-start.3 = (f32[6,2048]{1,0:T(8,128)S(1)}, f32[6,2048]{1,0:T(8,128)}, u32[]{:S(2)}) copy-start(f32[6,2048]{1,0:T(8,128)} %circ_ref.3) | copy-start | bytes 147460
  19.3 6.4 %copy-start.5 = (s32[1,1,96,4]{2,3,1,0:T(4,128)S(1)}, s32[1,1,96,4]{2,3,1,0:T(4,128)}, u32[]{:S(2)}) copy-start(s32[1,1,96,4]{2,3,1,0:T(4,128)} %param.11) | copy-start | bytes 4612
  19.3 25.9 %all-to-all-start = ((f32[32,40,128]{2,1,0:T(8,128)}), f32[32,40,128]{2,1,0:T(8,128)S(1)}, u32[]{:S(2)}, u32[]{:S(2)}) async-start(f32[32,40,128]{2,1,0:T(8,128)} %shard_map.77), calls=%async_computation | async-start | bytes 1310720 | tf_op jit(solution)/shard_map/all_to_all | solution.py:270
  25.6 0.7 %copy-start.4 = (s32[1,1,96,8]{2,3,1,0:T(8,128)S(1)}, s32[1,1,96,8]{2,3,1,0:T(8,128)}, u32[]{:S(2)}) copy-start(s32[1,1,96,8]{2,3,1,0:T(8,128)} %param.9) | copy-start | bytes 9220
  25.6 0.7 %copy-start.6 = (s32[1,1,96]{2,1,0:T(1,128)S(1)}, s32[1,1,96]{2,1,0:T(1,128)}, u32[]{:S(2)}) copy-start(s32[1,1,96]{2,1,0:T(1,128)} %param.10) | copy-start | bytes 1156

commit v3 on v2

--- a/solution.py
+++ b/solution.py
@@ -29,26 +29,12 @@
     return first, second, third
 
 
-def lattice(pos_ref, circ_ref, next_ref, last_ref):
-    ends = last_ref[0] == 1
-    middles, strengths = [], []
-    for comp in range(3):
-        here = pos_ref[comp]
-        beyond = jnp.where(ends, here[:, -SPAN:], next_ref[comp])
-        segment = jnp.concatenate([here[:, SPAN:], beyond], axis=1) - here
-        middles.append(here + 0.5 * segment)
-        strengths.append(circ_ref[...] * segment)
-    return middles, strengths
-
-
 def source_rows(middle, strength):
-    near_rows = []
-    for comp in range(3):
-        m1, m2, m3 = split3(-2.0 * middle[comp])
-        near_rows += [m1, m2, m1, m2, m3, m1]
+    parts = [split3(-2.0 * middle[comp]) for comp in range(3)]
     square = middle[0] * middle[0] + middle[1] * middle[1] + middle[2] * middle[2] + core_square
-    zero = jnp.zeros_like(square)
-    near_rows += [jnp.ones_like(square)] * 3 + list(split3(square)) + [zero] * 8
+    squares = split3(square)
+    near_rows = [parts[comp][0] for comp in range(3)] + [parts[comp][1] for comp in range(3)]
+    near_rows += [squares[0], squares[1]] + [parts[comp][2] for comp in range(3)] + [squares[2]]
     w1, w2, w = [], [], []
     for comp in range(3):
         first, second, _ = split3(inv_four_pi * strength[comp])
@@ -60,34 +46,108 @@
         split3(w[2] * middle[0] - w[0] * middle[2]),
         split3(w[0] * middle[1] - w[1] * middle[0]),
     ]
-    strength_rows = w1 + w2 + [u[comp][level] for level in range(3) for comp in range(3)] + [zero]
+    strength_rows = w1 + w2 + [u[comp][level] for level in range(3) for comp in range(3)]
     return near_rows, strength_rows
 
 
 def target_rows(point):
-    rows = []
+    parts = [split3(point[comp]) for comp in range(3)]
+    square = point[0] * point[0] + point[1] * point[1] + point[2] * point[2]
+    one, zero = jnp.ones_like(square), jnp.zeros_like(square)
+    first, second, third = ([parts[comp][level] for comp in range(3)] for level in range(3))
+    return (
+        first + first + [one, one]
+        + second + second + [zero, zero]
+        + third + [zero] * 5
+        + first + [one] + list(split3(square)) + [zero]
+    )
+
+
+def fixed_rows(blocks, stage):
+    line = lax.broadcasted_iota(jnp.int32, (8, TILE), 0)
+    ones = jnp.where((line >= 4) & (line < 7), 1.0, 0.0)
+
+    def fill(b, _):
+        stage[pl.ds(pl.multiple_of(b * DEPTH + 8, 8), 8), :] = ones
+        stage[pl.ds(pl.multiple_of(b * DEPTH + 24, 8), 8), :] = jnp.zeros_like(ones)
+        return 0
+
+    lax.fori_loop(0, blocks, fill, 0, unroll=8)
+
+
+def pack_sources(blocks, stage, st, ww):
+    def pack(b, _):
+        base = pl.multiple_of(b * DEPTH, DEPTH)
+        top = stage[pl.ds(base, 8), :]
+        rest = stage[pl.ds(base + 8, 8), :]
+        st[b] = jnp.concatenate([top, top, top, rest], axis=0).T.astype(BF16)
+        ww[b] = stage[pl.ds(base + 16, SUMS), :].astype(BF16)
+        return 0
+
+    lax.fori_loop(0, blocks, pack, 0, unroll=8)
+
+
+def source_lines(near_rows, strength_rows):
+    return list(enumerate(near_rows)) + [(16 + r, row) for r, row in enumerate(strength_rows)]
+
+
+def first_kernel(
+    rows, halves, kmax, pos_ref, circ_ref, slot_ref, count_ref, field_ref, tt_ref, item_ref, total_ref, stage
+):
+    tiles = rows * halves
+    points = [pos_ref[comp] for comp in range(3)]
     for comp in range(3):
-        x1, x2, x3 = split3(point[comp])
-        rows += [x1, x1, x2, x2, x1, x3]
-    square = point[0] * point[0] + point[1] * point[1] + point[2] * point[2]
-    rows += list(split3(square)) + [jnp.ones_like(square)] * 3 + [jnp.zeros_like(square)] * 8
-    return rows
-
-
-def send_kernel(rows, halves, peers, cap, pos_ref, circ_ref, next_ref, last_ref, list_ref, out_ref, stage):
-    middles, strengths = lattice(pos_ref, circ_ref, next_ref, last_ref)
-    for comp, field in enumerate(middles + strengths):
+        here = points[comp]
+        segment = jnp.concatenate([here[:, SPAN:], here[:, -SPAN:]], axis=1) - here
+        middle = here + 0.5 * segment
+        strength = circ_ref[...] * segment
         for half in range(halves):
-            stage[pl.ds(half * 8 + comp, rows, halves * 8), :] = field[:, half * TILE : (half + 1) * TILE]
+            cut = slice(half * TILE, (half + 1) * TILE)
+            field_ref[pl.ds(half * 8 + comp, rows, halves * 8), :] = middle[:, cut]
+            field_ref[pl.ds(half * 8 + 3 + comp, rows, halves * 8), :] = strength[:, cut]
+    for r, field in enumerate(target_rows(points)):
+        for half in range(halves):
+            stage[pl.ds(half * DEPTH + r, rows, halves * DEPTH), :] = field[:, half * TILE : (half + 1) * TILE]
+
+    def pack(b, _):
+        tt_ref[b] = stage[pl.ds(pl.multiple_of(b * DEPTH, DEPTH), DEPTH), :].astype(BF16)
+        return 0
+
+    lax.fori_loop(0, tiles, pack, 0, unroll=8)
+
+    def listed(b, at):
+        for k in range(kmax):
+            item_ref[at + k] = b * 256 + slot_ref[k, b]
+        return at + count_ref[b]
+
+    total = lax.fori_loop(0, tiles, listed, 0)
+    for k in range((STEPS + 2) * GROUP):
+        item_ref[total + k] = tiles * 256
+    total_ref[0] = total
+
+
+def send_kernel(rows, halves, peers, cap, field_ref, pos_ref, circ_ref, next_ref, last_ref, list_ref, out_ref, full_ref):
+    full_ref[...] = field_ref[...]
+
+    @pl.when(last_ref[0] == 0)
+    def _():
+        width = halves * TILE
+        circ = circ_ref[:, width - TILE :]
+        for comp in range(3):
+            here = pos_ref[comp, :, width - TILE :]
+            segment = jnp.concatenate([here[:, SPAN:], next_ref[comp]], axis=1) - here
+            at = (halves - 1) * 8 + comp
+            full_ref[pl.ds(at, rows, halves * 8), :] = here + 0.5 * segment
+            full_ref[pl.ds(at + 3, rows, halves * 8), :] = circ * segment
 
     def fill(peer, _):
         for c in range(cap):
             block = list_ref[c, 0, peer]
-            data = stage[pl.ds(pl.multiple_of(block * 8, 8), 8), :]
+            data = full_ref[pl.ds(pl.multiple_of(block * 8, 8), 8), :]
             out_ref[peer, c * 6 : c * 6 + 6, :] = data[:6]
         return 0
 
-    lax.fori_loop(0, peers, fill, 0)
+    lax.fori_loop(0, peers, fill, 0, unroll=2)
 
 
 def interact(count, item, tt, st, ww, acc, dsc, ksc):
@@ -136,45 +196,14 @@
     lax.fori_loop(0, count, turn, 0)
 
 
-def near_kernel(
-    rows, halves, near, kmax,
-    pos_ref, circ_ref, next_ref, last_ref, near_ref, slot_ref, count_ref,
-    tt_ref, acc_ref, item_ref, total_ref,
-    st, ww, stage, dsc, ksc,
-):
+def near_kernel(rows, halves, near, full_ref, tt_ref, near_ref, acc_ref, st, ww, stage, dsc, ksc):
     tiles = rows * halves
-    middles, strengths = lattice(pos_ref, circ_ref, next_ref, last_ref)
-    points = [pos_ref[comp] for comp in range(3)]
-    deep = 2 * DEPTH + SUMS
-
-    def lay(fields, start):
-        for half in range(halves):
-            cut = slice(half * TILE, (half + 1) * TILE)
-            for r, field in enumerate(fields):
-                stage[pl.ds(half * deep + start + r, rows, halves * deep), :] = field[:, cut]
-
-    near_rows, strength_rows = source_rows(middles, strengths)
-    lay(near_rows + target_rows(points) + strength_rows, 0)
-
-    def pack(b, _):
-        base = pl.multiple_of(b * deep, SUMS)
-        st[b] = stage[pl.ds(base, DEPTH), :].T.astype(BF16)
-        tt_ref[b] = stage[pl.ds(base + DEPTH, DEPTH), :].astype(BF16)
-        ww[b] = stage[pl.ds(base + 2 * DEPTH, SUMS), :].astype(BF16)
-        return 0
-
-    lax.fori_loop(0, tiles, pack, 0, unroll=8)
-
-    def listed(b, at):
-        for k in range(kmax):
-            item_ref[at + k] = b * 256 + slot_ref[k, b]
-        return at + count_ref[b]
-
-    total = lax.fori_loop(0, tiles, listed, 0)
-    for k in range((STEPS + 2) * GROUP):
-        item_ref[total + k] = tiles * 256
-    total_ref[0] = total
-
+    fixed_rows(tiles, stage)
+    for half in range(halves):
+        parts = [full_ref[pl.ds(half * 8 + comp, rows, halves * 8), :] for comp in range(6)]
+        for r, field in source_lines(*source_rows(parts[:3], parts[3:])):
+            stage[pl.ds(half * DEPTH + r, rows, halves * DEPTH), :] = field
+    pack_sources(tiles, stage, st, ww)
     last = tiles * near - 1
 
     def item(i):
@@ -192,27 +221,19 @@
     vel_ref, moved_ref,
     st, ww, stage, acc, dsc, ksc,
 ):
-    deep = DEPTH + SUMS
+    fixed_rows(peers * cap, stage)
 
     def lay(group, _):
         for c in range(cap):
             parts = [
                 recv_ref[pl.ds(group * (8 * width_rows) + c * 6 + comp, 8, width_rows), :] for comp in range(6)
             ]
-            near_rows, strength_rows = source_rows(parts[:3], parts[3:])
-            for r, field in enumerate(near_rows + strength_rows):
-                stage[pl.ds(group * (8 * cap * deep) + c * deep + r, 8, cap * deep), :] = field
+            for r, field in source_lines(*source_rows(parts[:3], parts[3:])):
+                stage[pl.ds(group * (8 * cap * DEPTH) + c * DEPTH + r, 8, cap * DEPTH), :] = field
         return 0
 
     lax.fori_loop(0, peers // 8, lay, 0)
-
-    def pack(b, _):
-        base = pl.multiple_of(b * deep, SUMS)
-        st[b] = stage[pl.ds(base, DEPTH), :].T.astype(BF16)
-        ww[b] = stage[pl.ds(base + DEPTH, SUMS), :].astype(BF16)
-        return 0
-
-    lax.fori_loop(0, peers * cap, pack, 0, unroll=8)
+    pack_sources(peers * cap, stage, st, ww)
 
     def item(i):
         code = item_ref[i]
@@ -259,39 +280,50 @@
     width_rows = -(-cap * 6 // 8) * 8
     params = pltpu.CompilerParams(vmem_limit_bytes=48 << 20)
 
-    outgoing = pl.pallas_call(
+    fields, targets, items, total = pl.pallas_call(
+        functools.partial(first_kernel, rows, halves, kmax),
+        out_shape=(
+            jax.ShapeDtypeStruct((tiles * 8, TILE), F32),
+            jax.ShapeDtypeStruct((tiles, DEPTH, TILE), BF16),
+            jax.ShapeDtypeStruct((tiles * kmax + 64,), jnp.int32),
+            jax.ShapeDtypeStruct((1,), jnp.int32),
+        ),
+        in_specs=[vmem, vmem, smem, smem],
+        out_specs=(vmem, vmem, smem, smem),
+        scratch_shapes=[pltpu.VMEM((tiles * DEPTH, TILE), F32)],
+        compiler_params=params,
+        cost_estimate=pl.CostEstimate(flops=10**8, bytes_accessed=2 << 20, transcendentals=0),
+    )(positions, circulation, reader_slots[0, 0].T, source_counts[0, 0])
+    outgoing, full = pl.pallas_call(
         functools.partial(send_kernel, rows, halves, peers, cap),
-        out_shape=jax.ShapeDtypeStruct((peers, width_rows, TILE), F32),
-        in_specs=[vmem, vmem, vmem, smem, smem],
-        out_specs=vmem,
-        scratch_shapes=[pltpu.VMEM((tiles * 8, TILE), F32)],
+        out_shape=(
+            jax.ShapeDtypeStruct((peers, width_rows, TILE), F32),
+            jax.ShapeDtypeStruct((tiles * 8, TILE), F32),
+        ),
+        in_specs=[vmem, vmem, vmem, vmem, smem, smem],
+        out_specs=(vmem, vmem),
         compiler_params=params,
-    )(positions, circulation, next_row, last, send_lists[0, 0].T[:, None])
+    )(fields, positions, circulation, next_row, last, send_lists[0, 0].T[:, None])
     incoming = lax.all_to_all(outgoing, "turb", 0, 0, tiled=True).reshape(peers * width_rows, TILE)
 
     pairs = [
         pltpu.VMEM((2, GROUP // 2, TILE, 2 * TILE), F32),
         pltpu.VMEM((2, GROUP // 2, 2 * TILE, 2 * TILE), BF16),
     ]
-    targets, near_acc, items, total = pl.pallas_call(
-        functools.partial(near_kernel, rows, halves, near, kmax),
-        out_shape=(
-            jax.ShapeDtypeStruct((tiles, DEPTH, TILE), BF16),
-            jax.ShapeDtypeStruct((tiles * SUMS, TILE), F32),
-            jax.ShapeDtypeStruct((tiles * kmax + 64,), jnp.int32),
-            jax.ShapeDtypeStruct((1,), jnp.int32),
-        ),
-        in_specs=[vmem, vmem, vmem, smem, smem, smem, smem],
-        out_specs=(vmem, vmem, smem, smem),
+    near_acc = pl.pallas_call(
+        functools.partial(near_kernel, rows, halves, near),
+        out_shape=jax.ShapeDtypeStruct((tiles * SUMS, TILE), F32),
+        in_specs=[vmem, vmem, smem],
+        out_specs=vmem,
         scratch_shapes=[
             pltpu.VMEM((tiles, TILE, DEPTH), BF16),
             pltpu.VMEM((tiles, SUMS, TILE), BF16),
-            pltpu.VMEM((tiles * (2 * DEPTH + SUMS), TILE), F32),
+            pltpu.VMEM((tiles * DEPTH, TILE), F32),
             *pairs,
         ],
         compiler_params=params,
         cost_estimate=pl.CostEstimate(flops=2 * 10**9, bytes_accessed=4 << 20, transcendentals=tiles * near * TILE * TILE),
-    )(positions, circulation, next_row, last, near_blocks[0, 0].T, reader_slots[0, 0].T, source_counts[0, 0])
+    )(full, targets, near_blocks[0, 0].T)
     return pl.pallas_call(
         functools.partial(far_kernel, rows, halves, peers, cap, width_rows),
         out_shape=(
@@ -303,7 +335,7 @@
         scratch_shapes=[
             pltpu.VMEM((peers * cap, TILE, DEPTH), BF16),
             pltpu.VMEM((peers * cap, SUMS, TILE), BF16),
-            pltpu.VMEM((peers * cap * (DEPTH + SUMS), TILE), F32),
+            pltpu.VMEM((peers * cap * DEPTH, TILE), F32),
             pltpu.VMEM(((tiles + 1) * SUMS, TILE), F32),
             *pairs,
         ],

time: 68.2 us -> 69.3 us (1.016)
  the two profiles are of different devices: /device:TPU:2 before, /device:TPU:7 now
where the time goes in v3:
time: 69.3 us; the launch traced here: 68.9 us
  Pallas kernels  38.6 us (56%)
  starting transfers between devices  19.7 us (28%)
  waiting for transfers between devices  5.46 us (8%)
  local copies, waits for them, and re-layouts  4.5 us (6%)
  between operations  0.73 us (1%)
    pallas_call x1, Pallas kernels, body(): pl.pallas_call(functools.partial(far_kernel, rows, halves, peers, cap, wi...  18.8 us
    pallas_call x1, Pallas kernels, body(): pl.pallas_call(functools.partial(near_kernel, rows, halves, near), out_sh...  13.4 us
    ppermute x1, starting transfers between devices, body(): lax.ppermute(positions[:, :, :SPAN], 'age', [(s, s - 1) for s in range(1,...  12.7 us
    all_to_all x1, starting transfers between devices, body(): lax.all_to_all(outgoing, 'turb', 0, 0, tiled=True)  6.94 us
    all_to_all x1, waiting for transfers between devices, body(): lax.all_to_all(outgoing, 'turb', 0, 0, tiled=True)  5.45 us
    pallas_call x1, Pallas kernels, body(): pl.pallas_call(functools.partial(first_kernel, rows, halves, kmax), out_s...  4.47 us
    unnamed x17, local copies, waits for them, and re-layouts  3.77 us
    pallas_call x1, Pallas kernels, body(): pl.pallas_call(functools.partial(send_kernel, rows, halves, peers, cap),...  1.85 us
  transfers between devices with their start and end apart: 2, of which 1 were waited for; matrix products, arithmetic and copies ran while one was open for 0% of the time, Pallas kernels for 26%

profile of v3, /device:TPU:7, one launch (start us, length us, event | category | flops | bytes accessed | tf_op | source)
XLA Modules:
  0.0 68.9 jit_solution(5689608019375191748)
XLA Ops:
  0.6 0.0 copy-start.4
  0.6 0.7 %slice.3 = f32[3,6,64]{2,1,0:T(8,128)S(1)} slice(f32[3,6,2048]{2,1,0:T(8,128)} %pos_ref.5), slice={[0:3], [0:6], [0:64]} | slice | bytes 9216 | tf_op jit(solution)/shard_map/slice | solution.py:278
  1.4 12.7 %collective-permute-start = (f32[3,6,64]{2,1,0:T(8,128)S(1)}, f32[3,6,64]{2,1,0:T(8,128)S(1)}, u32[]{:S(2)}, u32[]{:S(2)}) collective-permute-start(f32[3,6,64]{2,1,0:T(8,128)S(1)} %slice.3), channel_id=1, source_target_pairs={{1,0},{2,1},{3,2},{4,3},{5,4},{6,5},{7,6},{8,7},{9,8},{10,9},{11,1... | collective-permute-start | bytes 13832 | tf_op jit(solution)/shard_map/ppermute | solution.py:278
  14.1 0.0 copy-start.6
  14.1 0.0 copy-done.4
  14.1 0.6 copy-done.6
  14.7 0.0 copy-start
  14.7 0.9 %copy-done = f32[3,6,2048]{2,1,0:T(8,128)S(1)} copy-done((f32[3,6,2048]{2,1,0:T(8,128)S(1)}, f32[3,6,2048]{2,1,0:T(8,128)}, u32[]{:S(2)}) %copy-start) | copy-done | bytes 147480
  15.7 0.0 copy-start.2
  15.7 0.8 %copy-done.2 = f32[6,2048]{1,0:T(8,128)S(1)} copy-done((f32[6,2048]{1,0:T(8,128)S(1)}, f32[6,2048]{1,0:T(8,128)}, u32[]{:S(2)}) %copy-start.2) | copy-done | bytes 49176
  16.5 0.0 copy-start.1
  16.5 0.0 copy-start.3
  16.5 4.5 %shard_map.77 = (f32[768,128]{1,0:T(8,128)S(1)}, bf16[96,32,128]{2,1,0:T(8,128)(2,1)S(1)}, s32[832]{0:T(1024)S(1)}, s32[1]{0:T(128)}) custom-call(f32[3,6,2048]{2,1,0:T(8,128)S(1)} %copy-done, f32[6,2048]{1,0:T(8,128)S(1)} %copy-done.2, s32[8,96]{1,0:T(8,128)S(1)} %bitcast.15, s32[96]{0:T(128)S(1)} %bitcast.17), custom_call_target="tpu_custom_call" | custom-call | flops 100000000 | bytes 2097152 | tf_op jit(solution)/shard_map/pallas_call | solution.py:283
  21.0 0.0 copy-start.7
  21.0 0.7 copy-done.7
  21.7 0.0 collective-permute-done.next_ref
  21.7 0.0 copy-done.1
  21.7 0.0 copy-done.3
  21.7 1.9 %shard_map.78 = (f32[32,40,128]{2,1,0:T(8,128)}, f32[768,128]{1,0:T(8,128)S(1)}) custom-call(f32[768,128]{1,0:T(8,128)S(1)} %get-tuple-element.8.field_ref, f32[3,6,2048]{2,1,0:T(8,128)S(1)} %copy-done.1, f32[6,2048]{1,0:T(8,128)S(1)} %copy-done.3, f32[3,6,64]{2,1,0:T(8,128)S(1)} %collective-permute-done.next_ref, s32[1]{0:T(128)} %bitcast.3.last_ref, ...), custom_call_target="tpu_custom_call" | custom-call | tf_op jit(solution)/shard_map/pallas_call | solution.py:297
  23.6 6.9 %all-to-all-start = ((f32[32,40,128]{2,1,0:T(8,128)}), f32[32,40,128]{2,1,0:T(8,128)S(1)}, u32[]{:S(2)}, u32[]{:S(2)}) async-start(f32[32,40,128]{2,1,0:T(8,128)} %get-tuple-element.9), calls=%async_computation | async-start | bytes 1310720 | tf_op jit(solution)/shard_map/all_to_all | solution.py:307
  30.5 0.0 copy-start.5
  30.5 0.7 copy-done.5
  31.2 13.4 %shard_map.79.near_acc = f32[1536,128]{1,0:T(8,128)S(1)} custom-call(f32[768,128]{1,0:T(8,128)S(1)} %get-tuple-element.11.full_ref, bf16[96,32,128]{2,1,0:T(8,128)(2,1)S(1)} %get-tuple-element.10.tt_ref, s32[4,96]{1,0:T(4,128)S(1)} %bitcast.16), custom_call_target="tpu_custom_call" | custom-call | flops 2000000000 | bytes 4194304 | tf_op jit(solution)/shard_map/pallas_call | solution.py:313
  44.6 5.5 %all-to-all-done = f32[32,40,128]{2,1,0:T(8,128)S(1)} async-done(((f32[32,40,128]{2,1,0:T(8,128)}), f32[32,40,128]{2,1,0:T(8,128)S(1)}, u32[]{:S(2)}, u32[]{:S(2)}) %all-to-all-start) | async-done | bytes 655392 | tf_op jit(solution)/shard_map/all_to_all | solution.py:307
  50.1 18.8 %shard_map.80 = (f32[3,6,2048]{2,1,0:T(8,128)}, f32[3,6,2048]{2,1,0:T(8,128)}) custom-call(f32[3,6,2048]{2,1,0:T(8,128)S(1)} %copy-done.1, f32[1280,128]{1,0:T(8,128)S(1)} %bitcast.14, bf16[96,32,128]{2,1,0:T(8,128)(2,1)S(1)} %get-tuple-element.10.tt_ref, f32[1536,128]{1,0:T(8,128)S(1)} %shard_map.79.near_acc, s32[832]{0:T(1024)S(1)} %get-tuple-element.12.item_ref, ...), custom_call_target="tpu_custom_call" | custom-call | tf_op jit(solution)/shard_map/pallas_call | solution.py:327
  (2 shorter events, 0.0 us)
Async XLA Ops:
  0.6 13.5 %copy-start.4 = (s32[1,1,96,8]{2,3,1,0:T(8,128)S(1)}, s32[1,1,96,8]{2,3,1,0:T(8,128)}, u32[]{:S(2)}) copy-start(s32[1,1,96,8]{2,3,1,0:T(8,128)} %param.9) | copy-start | bytes 9220
  1.4 20.3 %collective-permute-start = (f32[3,6,64]{2,1,0:T(8,128)S(1)}, f32[3,6,64]{2,1,0:T(8,128)S(1)}, u32[]{:S(2)}, u32[]{:S(2)}) collective-permute-start(f32[3,6,64]{2,1,0:T(8,128)S(1)} %slice.3), channel_id=1, source_target_pairs={{1,0},{2,1},{3,2},{4,3},{5,4},{6,5},{7,6},{8,7},{9,8},{10,9},{11,1... | collective-permute-start | bytes 13832 | tf_op jit(solution)/shard_map/ppermute | solution.py:278
  14.1 0.7 copy-start.6
  14.7 0.9 %copy-start = (f32[3,6,2048]{2,1,0:T(8,128)S(1)}, f32[3,6,2048]{2,1,0:T(8,128)}, u32[]{:S(2)}) copy-start(f32[3,6,2048]{2,1,0:T(8,128)} %pos_ref.5) | copy-start | bytes 442372
  15.7 0.8 %copy-start.2 = (f32[6,2048]{1,0:T(8,128)S(1)}, f32[6,2048]{1,0:T(8,128)}, u32[]{:S(2)}) copy-start(f32[6,2048]{1,0:T(8,128)} %circ_ref.3) | copy-start | bytes 147460
  16.5 5.2 %copy-start.1 = (f32[3,6,2048]{2,1,0:T(8,128)S(1)}, f32[3,6,2048]{2,1,0:T(8,128)}, u32[]{:S(2)}) copy-start(f32[3,6,2048]{2,1,0:T(8,128)} %pos_ref.5) | copy-start | bytes 442372
  16.5 5.2 %copy-start.3 = (f32[6,2048]{1,0:T(8,128)S(1)}, f32[6,2048]{1,0:T(8,128)}, u32[]{:S(2)}) copy-start(f32[6,2048]{1,0:T(8,128)} %circ_ref.3) | copy-start | bytes 147460
  21.0 0.7 copy-start.7
  23.6 26.5 %all-to-all-start = ((f32[32,40,128]{2,1,0:T(8,128)}), f32[32,40,128]{2,1,0:T(8,128)S(1)}, u32[]{:S(2)}, u32[]{:S(2)}) async-start(f32[32,40,128]{2,1,0:T(8,128)} %get-tuple-element.9), calls=%async_computation | async-start | bytes 1310720 | tf_op jit(solution)/shard_map/all_to_all | solution.py:307
  30.5 0.7 copy-start.5

commit v4 on v3

--- a/solution.py
+++ b/solution.py
@@ -91,60 +91,34 @@
     return list(enumerate(near_rows)) + [(16 + r, row) for r, row in enumerate(strength_rows)]
 
 
-def first_kernel(
-    rows, halves, kmax, pos_ref, circ_ref, slot_ref, count_ref, field_ref, tt_ref, item_ref, total_ref, stage
+def send_kernel(
+    rows, halves, peers, cap, pos_hbm, circ_hbm, next_ref, last_ref, list_ref, out_ref, full_ref, pos_ref, circ_ref, sems
 ):
-    tiles = rows * halves
-    points = [pos_ref[comp] for comp in range(3)]
+    copies = [
+        pltpu.make_async_copy(pos_hbm, pos_ref, sems.at[0]),
+        pltpu.make_async_copy(circ_hbm, circ_ref, sems.at[1]),
+    ]
+    for copy in copies:
+        copy.start()
+    for copy in copies:
+        copy.wait()
+    ends = last_ref[0] == 1
     for comp in range(3):
-        here = points[comp]
-        segment = jnp.concatenate([here[:, SPAN:], here[:, -SPAN:]], axis=1) - here
+        here = pos_ref[comp]
+        beyond = jnp.where(ends, here[:, -SPAN:], next_ref[comp])
+        segment = jnp.concatenate([here[:, SPAN:], beyond], axis=1) - here
         middle = here + 0.5 * segment
         strength = circ_ref[...] * segment
         for half in range(halves):
             cut = slice(half * TILE, (half + 1) * TILE)
-            field_ref[pl.ds(half * 8 + comp, rows, halves * 8), :] = middle[:, cut]
-            field_ref[pl.ds(half * 8 + 3 + comp, rows, halves * 8), :] = strength[:, cut]
-    for r, field in enumerate(target_rows(points)):
-        for half in range(halves):
-            stage[pl.ds(half * DEPTH + r, rows, halves * DEPTH), :] = field[:, half * TILE : (half + 1) * TILE]
-
-    def pack(b, _):
-        tt_ref[b] = stage[pl.ds(pl.multiple_of(b * DEPTH, DEPTH), DEPTH), :].astype(BF16)
-        return 0
-
-    lax.fori_loop(0, tiles, pack, 0, unroll=8)
-
-    def listed(b, at):
-        for k in range(kmax):
-            item_ref[at + k] = b * 256 + slot_ref[k, b]
-        return at + count_ref[b]
-
-    total = lax.fori_loop(0, tiles, listed, 0)
-    for k in range((STEPS + 2) * GROUP):
-        item_ref[total + k] = tiles * 256
-    total_ref[0] = total
-
-
-def send_kernel(rows, halves, peers, cap, field_ref, pos_ref, circ_ref, next_ref, last_ref, list_ref, out_ref, full_ref):
-    full_ref[...] = field_ref[...]
-
-    @pl.when(last_ref[0] == 0)
-    def _():
-        width = halves * TILE
-        circ = circ_ref[:, width - TILE :]
-        for comp in range(3):
-            here = pos_ref[comp, :, width - TILE :]
-            segment = jnp.concatenate([here[:, SPAN:], next_ref[comp]], axis=1) - here
-            at = (halves - 1) * 8 + comp
-            full_ref[pl.ds(at, rows, halves * 8), :] = here + 0.5 * segment
-            full_ref[pl.ds(at + 3, rows, halves * 8), :] = circ * segment
+            full_ref[pl.ds(half * 8 + comp, rows, halves * 8), :] = middle[:, cut]
+            full_ref[pl.ds(half * 8 + 3 + comp, rows, halves * 8), :] = strength[:, cut]
 
     def fill(peer, _):
         for c in range(cap):
             block = list_ref[c, 0, peer]
             data = full_ref[pl.ds(pl.multiple_of(block * 8, 8), 8), :]
-            out_ref[peer, c * 6 : c * 6 + 6, :] = data[:6]
+            out_ref[pl.ds(peer * (cap * 6) + c * 6, 6), :] = data[:6]
         return 0
 
     lax.fori_loop(0, peers, fill, 0, unroll=2)
@@ -196,8 +170,31 @@
     lax.fori_loop(0, count, turn, 0)
 
 
-def near_kernel(rows, halves, near, full_ref, tt_ref, near_ref, acc_ref, st, ww, stage, dsc, ksc):
+def near_kernel(
+    rows, halves, near, kmax, pos_ref, full_ref, near_ref, slot_ref, count_ref,
+    acc_ref, tt_ref, item_ref, total_ref, st, ww, stage, dsc, ksc,
+):
     tiles = rows * halves
+    for r, field in enumerate(target_rows([pos_ref[comp] for comp in range(3)])):
+        for half in range(halves):
+            stage[pl.ds(half * DEPTH + r, rows, halves * DEPTH), :] = field[:, half * TILE : (half + 1) * TILE]
+
+    def pack(b, _):
+        tt_ref[b] = stage[pl.ds(pl.multiple_of(b * DEPTH, DEPTH), DEPTH), :].astype(BF16)
+        return 0
+
+    lax.fori_loop(0, tiles, pack, 0, unroll=8)
+
+    def listed(b, at):
+        for k in range(kmax):
+            item_ref[at + k] = b * 256 + slot_ref[k, b]
+        return at + count_ref[b]
+
+    total = lax.fori_loop(0, tiles, listed, 0)
+    for k in range((STEPS + 2) * GROUP):
+        item_ref[total + k] = tiles * 256
+    total_ref[0] = total
+
     fixed_rows(tiles, stage)
     for half in range(halves):
         parts = [full_ref[pl.ds(half * 8 + comp, rows, halves * 8), :] for comp in range(6)]
@@ -277,44 +274,42 @@
     ages = lax.axis_size("age")
     next_row = lax.ppermute(positions[:, :, :SPAN], "age", [(s, s - 1) for s in range(1, ages)])
     last = (lax.axis_index("age") == ages - 1).astype(jnp.int32).reshape(1)
-    width_rows = -(-cap * 6 // 8) * 8
+    width_rows = cap * 6
     params = pltpu.CompilerParams(vmem_limit_bytes=48 << 20)
 
-    fields, targets, items, total = pl.pallas_call(
-        functools.partial(first_kernel, rows, halves, kmax),
+    anywhere = pl.BlockSpec(memory_space=pltpu.HBM)
+    outgoing, full = pl.pallas_call(
+        functools.partial(send_kernel, rows, halves, peers, cap),
         out_shape=(
+            jax.ShapeDtypeStruct((peers * width_rows, TILE), F32),
             jax.ShapeDtypeStruct((tiles * 8, TILE), F32),
+        ),
+        in_specs=[anywhere, anywhere, vmem, smem, smem],
+        out_specs=(vmem, vmem),
+        scratch_shapes=[
+            pltpu.VMEM(positions.shape, F32),
+            pltpu.VMEM(circulation.shape, F32),
+            pltpu.SemaphoreType.DMA((2,)),
+        ],
+        compiler_params=params,
+    )(positions, circulation, next_row, last, send_lists[0, 0].T[:, None])
+    incoming = lax.all_to_all(outgoing.reshape(peers, 1, width_rows * TILE), "turb", 0, 0, tiled=True)
+    incoming = incoming.reshape(peers * width_rows, TILE)
+
+    pairs = [
+        pltpu.VMEM((2, GROUP // 2, TILE, 2 * TILE), F32),
+        pltpu.VMEM((2, GROUP // 2, 2 * TILE, 2 * TILE), BF16),
+    ]
+    near_acc, targets, items, total = pl.pallas_call(
+        functools.partial(near_kernel, rows, halves, near, kmax),
+        out_shape=(
+            jax.ShapeDtypeStruct((tiles * SUMS, TILE), F32),
             jax.ShapeDtypeStruct((tiles, DEPTH, TILE), BF16),
             jax.ShapeDtypeStruct((tiles * kmax + 64,), jnp.int32),
             jax.ShapeDtypeStruct((1,), jnp.int32),
         ),
-        in_specs=[vmem, vmem, smem, smem],
+        in_specs=[vmem, vmem, smem, smem, smem],
         out_specs=(vmem, vmem, smem, smem),
-        scratch_shapes=[pltpu.VMEM((tiles * DEPTH, TILE), F32)],
-        compiler_params=params,
-        cost_estimate=pl.CostEstimate(flops=10**8, bytes_accessed=2 << 20, transcendentals=0),
-    )(positions, circulation, reader_slots[0, 0].T, source_counts[0, 0])
-    outgoing, full = pl.pallas_call(
-        functools.partial(send_kernel, rows, halves, peers, cap),
-        out_shape=(
-            jax.ShapeDtypeStruct((peers, width_rows, TILE), F32),
-            jax.ShapeDtypeStruct((tiles * 8, TILE), F32),
-        ),
-        in_specs=[vmem, vmem, vmem, vmem, smem, smem],
-        out_specs=(vmem, vmem),
-        compiler_params=params,
-    )(fields, positions, circulation, next_row, last, send_lists[0, 0].T[:, None])
-    incoming = lax.all_to_all(outgoing, "turb", 0, 0, tiled=True).reshape(peers * width_rows, TILE)
-
-    pairs = [
-        pltpu.VMEM((2, GROUP // 2, TILE, 2 * TILE), F32),
-        pltpu.VMEM((2, GROUP // 2, 2 * TILE, 2 * TILE), BF16),
-    ]
-    near_acc = pl.pallas_call(
-        functools.partial(near_kernel, rows, halves, near),
-        out_shape=jax.ShapeDtypeStruct((tiles * SUMS, TILE), F32),
-        in_specs=[vmem, vmem, smem],
-        out_specs=vmem,
         scratch_shapes=[
             pltpu.VMEM((tiles, TILE, DEPTH), BF16),
             pltpu.VMEM((tiles, SUMS, TILE), BF16),
@@ -323,7 +318,7 @@
         ],
         compiler_params=params,
         cost_estimate=pl.CostEstimate(flops=2 * 10**9, bytes_accessed=4 << 20, transcendentals=tiles * near * TILE * TILE),
-    )(full, targets, near_blocks[0, 0].T)
+    )(positions, full, near_blocks[0, 0].T, reader_slots[0, 0].T, source_counts[0, 0])
     return pl.pallas_call(
         functools.partial(far_kernel, rows, halves, peers, cap, width_rows),
         out_shape=(

time: 69.3 us -> 64.8 us (0.935)
  the two profiles are of different devices: /device:TPU:7 before, /device:TPU:1 now
where the time goes in v4:
time: 64.8 us; the launch traced here: 63.5 us
  Pallas kernels  38.4 us (59%)
  starting transfers between devices  11.7 us (18%)
  waiting for transfers between devices  8.9 us (14%)
  local copies, waits for them, and re-layouts  3.85 us (6%)
  between operations  0.72 us (1%)
    pallas_call x1, Pallas kernels, body(): pl.pallas_call(functools.partial(far_kernel, rows, halves, peers, cap, wi...  18.8 us
    pallas_call x1, Pallas kernels, body(): pl.pallas_call(functools.partial(near_kernel, rows, halves, near, kmax),...  17.3 us
    all_to_all x1, starting transfers between devices, body(): lax.all_to_all(outgoing.reshape(peers, 1, width_rows * TILE), 'turb', 0,...  10.4 us
    ppermute x1, waiting for transfers between devices, body(): lax.ppermute(positions[:, :, :SPAN], 'age', [(s, s - 1) for s in range(1,...  8.72 us
    unnamed x15, local copies, waits for them, and re-layouts  3.12 us
    pallas_call x1, Pallas kernels, body(): pl.pallas_call(functools.partial(send_kernel, rows, halves, peers, cap),...  2.3 us
  transfers between devices with their start and end apart: 2, of which 2 were waited for; matrix products, arithmetic and copies ran while one was open for 0% of the time, Pallas kernels for 27%

profile of v4, /device:TPU:1, one launch (start us, length us, event | category | flops | bytes accessed | tf_op | source)
XLA Modules:
  0.0 63.5 jit_solution(9631026765560729203)
XLA Ops:
  0.6 0.7 %slice.3 = f32[3,6,64]{2,1,0:T(8,128)S(1)} slice(f32[3,6,2048]{2,1,0:T(8,128)} %pos_ref.3), slice={[0:3], [0:6], [0:64]} | slice | bytes 9216 | tf_op jit(solution)/shard_map/slice | solution.py:275
  1.3 1.3 %collective-permute-start = (f32[3,6,64]{2,1,0:T(8,128)S(1)}, f32[3,6,64]{2,1,0:T(8,128)S(1)}, u32[]{:S(2)}, u32[]{:S(2)}) collective-permute-start(f32[3,6,64]{2,1,0:T(8,128)S(1)} %slice.3), channel_id=1, source_target_pairs={{1,0},{2,1},{3,2},{4,3},{5,4},{6,5},{7,6},{8,7},{9,8},{10,9},{11,1... | collective-permute-start | bytes 13832 | tf_op jit(solution)/shard_map/ppermute | solution.py:275
  2.6 0.0 copy-start.6
  2.7 0.7 %copy-done.6 = s32[1,1,32,6]{2,1,3,0:T(1,128)S(1)} copy-done((s32[1,1,32,6]{2,1,3,0:T(1,128)S(1)}, s32[1,1,32,6]{2,1,3,0:T(1,128)}, u32[]{:S(2)}) %copy-start.6) | copy-done | bytes 792
  3.3 8.7 %collective-permute-done.next_ref = f32[3,6,64]{2,1,0:T(8,128)S(1)} collective-permute-done((f32[3,6,64]{2,1,0:T(8,128)S(1)}, f32[3,6,64]{2,1,0:T(8,128)S(1)}, u32[]{:S(2)}, u32[]{:S(2)}) %collective-permute-start) | collective-permute-done | bytes 4640 | tf_op jit(solution)/shard_map/ppermute | solution.py:275
  12.1 0.0 copy-start
  12.1 0.9 %copy-done = f32[3,6,2048]{2,1,0:T(8,128)S(1)} copy-done((f32[3,6,2048]{2,1,0:T(8,128)S(1)}, f32[3,6,2048]{2,1,0:T(8,128)}, u32[]{:S(2)}) %copy-start) | copy-done | bytes 147480
  13.0 0.0 copy-start.2
  13.0 0.8 %copy-done.2 = f32[6,2048]{1,0:T(8,128)S(1)} copy-done((f32[6,2048]{1,0:T(8,128)S(1)}, f32[6,2048]{1,0:T(8,128)}, u32[]{:S(2)}) %copy-start.2) | copy-done | bytes 49176
  13.8 2.3 %shard_map.77 = (f32[1152,128]{1,0:T(8,128)}, f32[768,128]{1,0:T(8,128)S(1)}) custom-call(f32[3,6,2048]{2,1,0:T(8,128)S(1)} %copy-done, f32[6,2048]{1,0:T(8,128)S(1)} %copy-done.2, f32[3,6,64]{2,1,0:T(8,128)S(1)} %collective-permute-done.next_ref, s32[1]{0:T(128)} %bitcast.last_ref, s32[6,1,32]{2,1,0:T(1,128)S(1)} %broadcast_in_dim.3.list_ref), custom_call_target="tpu_custom_call" | custom-call | tf_op jit(solution)/shard_map/pallas_call | solution.py:281
  16.1 0.0 copy-start.1
  16.1 10.4 %all-to-all-start = ((f32[32,1,4608]{2,1,0:T(1,128)}), f32[32,1,4608]{2,1,0:T(1,128)S(1)}, u32[]{:S(2)}, u32[]{:S(2)}) async-start(f32[32,1,4608]{2,1,0:T(1,128)} %bitcast.2), calls=%async_computation | async-start | bytes 1179648 | tf_op jit(solution)/shard_map/all_to_all | solution.py:296
  26.5 0.0 copy-start.3
  26.5 0.0 copy-start.4
  26.6 0.0 copy-start.5
  26.6 0.0 copy-done.1
  26.6 0.6 %copy-done.3 = s32[1,1,96,8]{2,3,1,0:T(8,128)S(1)} copy-done((s32[1,1,96,8]{2,3,1,0:T(8,128)S(1)}, s32[1,1,96,8]{2,3,1,0:T(8,128)}, u32[]{:S(2)}) %copy-start.3) | copy-done | bytes 3096
  27.2 0.0 copy-done.4
  27.2 0.0 copy-done.5
  27.2 17.3 %shard_map.78 = (f32[1536,128]{1,0:T(8,128)S(1)}, bf16[96,32,128]{2,1,0:T(8,128)(2,1)S(1)}, s32[832]{0:T(1024)S(1)}, s32[1]{0:T(128)}) custom-call(f32[3,6,2048]{2,1,0:T(8,128)S(1)} %copy-done.1, f32[768,128]{1,0:T(8,128)S(1)} %get-tuple-element.9.full_ref, s32[4,96]{1,0:T(4,128)S(1)} %bitcast.17, s32[8,96]{1,0:T(8,128)S(1)} %bitcast.16, s32[96]{0:T(128)S(1)} %bitcast.18), custom_call_target="tpu_custom_call" | custom-call | flops 2000000000 | bytes 4194304 | tf_op jit(solution)/shard_map/pallas_call | solution.py:303
  44.5 0.2 all-to-all-done
  44.7 18.8 %shard_map.79 = (f32[3,6,2048]{2,1,0:T(8,128)}, f32[3,6,2048]{2,1,0:T(8,128)}) custom-call(f32[3,6,2048]{2,1,0:T(8,128)S(1)} %copy-done.1, f32[1152,128]{1,0:T(8,128)S(1)} %bitcast.15, bf16[96,32,128]{2,1,0:T(8,128)(2,1)S(1)} %get-tuple-element.10.tt_ref, f32[1536,128]{1,0:T(8,128)S(1)} %get-tuple-element.11.near_acc, s32[832]{0:T(1024)S(1)} %get-tuple-element.12.item_ref, ...), custom_call_target="tpu_custom_call" | custom-call | tf_op jit(solution)/shard_map/pallas_call | solution.py:322
  (2 shorter events, 0.0 us)
Async XLA Ops:
  1.3 10.7 %collective-permute-start = (f32[3,6,64]{2,1,0:T(8,128)S(1)}, f32[3,6,64]{2,1,0:T(8,128)S(1)}, u32[]{:S(2)}, u32[]{:S(2)}) collective-permute-start(f32[3,6,64]{2,1,0:T(8,128)S(1)} %slice.3), channel_id=1, source_target_pairs={{1,0},{2,1},{3,2},{4,3},{5,4},{6,5},{7,6},{8,7},{9,8},{10,9},{11,1... | collective-permute-start | bytes 13832 | tf_op jit(solution)/shard_map/ppermute | solution.py:275
  2.6 0.7 %copy-start.6 = (s32[1,1,32,6]{2,1,3,0:T(1,128)S(1)}, s32[1,1,32,6]{2,1,3,0:T(1,128)}, u32[]{:S(2)}) copy-start(s32[1,1,32,6]{2,1,3,0:T(1,128)} %param.8) | copy-start | bytes 2308
  12.1 0.9 %copy-start = (f32[3,6,2048]{2,1,0:T(8,128)S(1)}, f32[3,6,2048]{2,1,0:T(8,128)}, u32[]{:S(2)}) copy-start(f32[3,6,2048]{2,1,0:T(8,128)} %pos_ref.3) | copy-start | bytes 442372
  13.0 0.8 %copy-start.2 = (f32[6,2048]{1,0:T(8,128)S(1)}, f32[6,2048]{1,0:T(8,128)}, u32[]{:S(2)}) copy-start(f32[6,2048]{1,0:T(8,128)} %circ_hbm.1) | copy-start | bytes 147460
  16.1 10.4 %copy-start.1 = (f32[3,6,2048]{2,1,0:T(8,128)S(1)}, f32[3,6,2048]{2,1,0:T(8,128)}, u32[]{:S(2)}) copy-start(f32[3,6,2048]{2,1,0:T(8,128)} %pos_ref.3) | copy-start | bytes 442372
  16.1 28.6 %all-to-all-start = ((f32[32,1,4608]{2,1,0:T(1,128)}), f32[32,1,4608]{2,1,0:T(1,128)S(1)}, u32[]{:S(2)}, u32[]{:S(2)}) async-start(f32[32,1,4608]{2,1,0:T(1,128)} %bitcast.2), calls=%async_computation | async-start | bytes 1179648 | tf_op jit(solution)/shard_map/all_to_all | solution.py:296
  26.5 0.7 %copy-start.3 = (s32[1,1,96,8]{2,3,1,0:T(8,128)S(1)}, s32[1,1,96,8]{2,3,1,0:T(8,128)}, u32[]{:S(2)}) copy-start(s32[1,1,96,8]{2,3,1,0:T(8,128)} %param.9) | copy-start | bytes 9220
  26.5 0.7 %copy-start.4 = (s32[1,1,96,4]{2,3,1,0:T(4,128)S(1)}, s32[1,1,96,4]{2,3,1,0:T(4,128)}, u32[]{:S(2)}) copy-start(s32[1,1,96,4]{2,3,1,0:T(4,128)} %param.11) | copy-start | bytes 4612
  26.6 0.7 %copy-start.5 = (s32[1,1,96]{2,1,0:T(1,128)S(1)}, s32[1,1,96]{2,1,0:T(1,128)}, u32[]{:S(2)}) copy-start(s32[1,1,96]{2,1,0:T(1,128)} %param.10) | copy-start | bytes 1156

commit v5 on v4

--- a/solution.py
+++ b/solution.py
@@ -80,11 +80,11 @@
         base = pl.multiple_of(b * DEPTH, DEPTH)
         top = stage[pl.ds(base, 8), :]
         rest = stage[pl.ds(base + 8, 8), :]
-        st[b] = jnp.concatenate([top, top, top, rest], axis=0).T.astype(BF16)
+        st[b] = jnp.concatenate([top, top, top, rest], axis=0).astype(BF16).T
         ww[b] = stage[pl.ds(base + 16, SUMS), :].astype(BF16)
         return 0
 
-    lax.fori_loop(0, blocks, pack, 0, unroll=8)
+    lax.fori_loop(0, blocks, pack, 0, unroll=32)
 
 
 def source_lines(near_rows, strength_rows):
@@ -92,16 +92,8 @@
 
 
 def send_kernel(
-    rows, halves, peers, cap, pos_hbm, circ_hbm, next_ref, last_ref, list_ref, out_ref, full_ref, pos_ref, circ_ref, sems
+    rows, halves, peers, cap, pos_ref, circ_ref, next_ref, last_ref, list_ref, out_ref, full_ref
 ):
-    copies = [
-        pltpu.make_async_copy(pos_hbm, pos_ref, sems.at[0]),
-        pltpu.make_async_copy(circ_hbm, circ_ref, sems.at[1]),
-    ]
-    for copy in copies:
-        copy.start()
-    for copy in copies:
-        copy.wait()
     ends = last_ref[0] == 1
     for comp in range(3):
         here = pos_ref[comp]
@@ -116,7 +108,7 @@
 
     def fill(peer, _):
         for c in range(cap):
-            block = list_ref[c, 0, peer]
+            block = list_ref[0, c, 0, peer]
             data = full_ref[pl.ds(pl.multiple_of(block * 8, 8), 8), :]
             out_ref[pl.ds(peer * (cap * 6) + c * 6, 6), :] = data[:6]
         return 0
@@ -277,22 +269,16 @@
     width_rows = cap * 6
     params = pltpu.CompilerParams(vmem_limit_bytes=48 << 20)
 
-    anywhere = pl.BlockSpec(memory_space=pltpu.HBM)
     outgoing, full = pl.pallas_call(
         functools.partial(send_kernel, rows, halves, peers, cap),
         out_shape=(
             jax.ShapeDtypeStruct((peers * width_rows, TILE), F32),
             jax.ShapeDtypeStruct((tiles * 8, TILE), F32),
         ),
-        in_specs=[anywhere, anywhere, vmem, smem, smem],
+        in_specs=[vmem, vmem, vmem, smem, smem],
         out_specs=(vmem, vmem),
-        scratch_shapes=[
-            pltpu.VMEM(positions.shape, F32),
-            pltpu.VMEM(circulation.shape, F32),
-            pltpu.SemaphoreType.DMA((2,)),
-        ],
         compiler_params=params,
-    )(positions, circulation, next_row, last, send_lists[0, 0].T[:, None])
+    )(positions, circulation, next_row, last, send_lists.transpose(0, 3, 1, 2))
     incoming = lax.all_to_all(outgoing.reshape(peers, 1, width_rows * TILE), "turb", 0, 0, tiled=True)
     incoming = incoming.reshape(peers * width_rows, TILE)
 

time: 64.8 us -> 64 us (0.988); the launches traced: 63.5 us -> 63.6 us
  waiting for transfers between devices: 8.9 us -> 10.2 us
  local copies, waits for them, and re-layouts: 3.85 us -> 3.16 us
    ppermute x1, waiting for transfers between devices: 8.72 us -> 9.41 us  [body(): lax.ppermute(positions[:, :, :SPAN], 'age', [(s, s - 1) for s in range(1,...]
    unnamed x15 -> x14, local copies, waits for them, and re-layouts: 3.12 us -> 2.44 us
  transfers between devices with their start and end apart: 2 -> 2, of which waited for: 2 -> 2; matrix products, arithmetic and copies ran while one was open for 0% -> 0% of each run, Pallas kernels for 27% -> 26%
where the time goes in v5:
time: 64 us; the launch traced here: 63.6 us
  Pallas kernels  37.9 us (59%)
  starting transfers between devices  11.6 us (18%)
  waiting for transfers between devices  10.2 us (16%)
  local copies, waits for them, and re-layouts  3.16 us (5%)
  between operations  0.7 us (1%)
    pallas_call x1, Pallas kernels, body(): pl.pallas_call(functools.partial(far_kernel, rows, halves, peers, cap, wi...  19.3 us
    pallas_call x1, Pallas kernels, body(): pl.pallas_call(functools.partial(near_kernel, rows, halves, near, kmax),...  16.7 us
    all_to_all x1, starting transfers between devices, body(): lax.all_to_all(outgoing.reshape(peers, 1, width_rows * TILE), 'turb', 0,...  10.4 us
    ppermute x1, waiting for transfers between devices, body(): lax.ppermute(positions[:, :, :SPAN], 'age', [(s, s - 1) for s in range(1,...  9.41 us
    unnamed x14, local copies, waits for them, and re-layouts  2.44 us
    pallas_call x1, Pallas kernels, body(): pl.pallas_call(functools.partial(send_kernel, rows, halves, peers, cap),...  1.94 us
    ppermute x1, starting transfers between devices, body(): lax.ppermute(positions[:, :, :SPAN], 'age', [(s, s - 1) for s in range(1,...  1.28 us
  transfers between devices with their start and end apart: 2, of which 2 were waited for; matrix products, arithmetic and copies ran while one was open for 0% of the time, Pallas kernels for 26%

profile of v5, /device:TPU:1, one launch (start us, length us, event | category | flops | bytes accessed | tf_op | source)
XLA Modules:
  0.0 63.6 jit_solution(13940102618790682266)
XLA Ops:
  0.6 0.7 %slice.3 = f32[3,6,64]{2,1,0:T(8,128)S(1)} slice(f32[3,6,2048]{2,1,0:T(8,128)} %pos_ref.5), slice={[0:3], [0:6], [0:64]} | slice | bytes 9216 | tf_op jit(solution)/shard_map/slice | solution.py:267
  1.3 1.3 %collective-permute-start = (f32[3,6,64]{2,1,0:T(8,128)S(1)}, f32[3,6,64]{2,1,0:T(8,128)S(1)}, u32[]{:S(2)}, u32[]{:S(2)}) collective-permute-start(f32[3,6,64]{2,1,0:T(8,128)S(1)} %slice.3), channel_id=1, source_target_pairs={{1,0},{2,1},{3,2},{4,3},{5,4},{6,5},{7,6},{8,7},{9,8},{10,9},{11,1... | collective-permute-start | bytes 13832 | tf_op jit(solution)/shard_map/ppermute | solution.py:267
  2.6 0.0 copy-start.3
  2.7 9.4 %collective-permute-done.next_ref = f32[3,6,64]{2,1,0:T(8,128)S(1)} collective-permute-done((f32[3,6,64]{2,1,0:T(8,128)S(1)}, f32[3,6,64]{2,1,0:T(8,128)S(1)}, u32[]{:S(2)}, u32[]{:S(2)}) %collective-permute-start) | collective-permute-done | bytes 4640 | tf_op jit(solution)/shard_map/ppermute | solution.py:267
  12.1 0.0 copy-done.3
  12.1 0.0 copy-start
  12.1 0.9 %copy-done = f32[3,6,2048]{2,1,0:T(8,128)S(1)} copy-done((f32[3,6,2048]{2,1,0:T(8,128)S(1)}, f32[3,6,2048]{2,1,0:T(8,128)}, u32[]{:S(2)}) %copy-start) | copy-done | bytes 147480
  13.0 0.0 copy-start.2
  13.0 0.8 %copy-done.2 = f32[6,2048]{1,0:T(8,128)S(1)} copy-done((f32[6,2048]{1,0:T(8,128)S(1)}, f32[6,2048]{1,0:T(8,128)}, u32[]{:S(2)}) %copy-start.2) | copy-done | bytes 49176
  13.8 1.9 %shard_map.77 = (f32[1152,128]{1,0:T(8,128)}, f32[768,128]{1,0:T(8,128)S(1)}) custom-call(f32[3,6,2048]{2,1,0:T(8,128)S(1)} %copy-done, f32[6,2048]{1,0:T(8,128)S(1)} %copy-done.2, f32[3,6,64]{2,1,0:T(8,128)S(1)} %collective-permute-done.next_ref, s32[1]{0:T(128)} %bitcast.last_ref, s32[1,6,1,32]{3,2,1,0:T(1,128)S(1)} %bitcast.12), custom_call_target="tpu_custom_call" | custom-call | tf_op jit(solution)/shard_map/pallas_call | solution.py:272
  15.8 0.0 copy-start.1
  15.8 10.4 %all-to-all-start = ((f32[32,1,4608]{2,1,0:T(1,128)}), f32[32,1,4608]{2,1,0:T(1,128)S(1)}, u32[]{:S(2)}, u32[]{:S(2)}) async-start(f32[32,1,4608]{2,1,0:T(1,128)} %bitcast.2), calls=%async_computation | async-start | bytes 1179648 | tf_op jit(solution)/shard_map/all_to_all | solution.py:282
  26.1 0.0 copy-start.4
  26.2 0.0 copy-start.5
  26.2 0.0 copy-start.6
  26.2 0.0 copy-done.1
  26.2 0.6 %copy-done.4 = s32[1,1,96,8]{2,3,1,0:T(8,128)S(1)} copy-done((s32[1,1,96,8]{2,3,1,0:T(8,128)S(1)}, s32[1,1,96,8]{2,3,1,0:T(8,128)}, u32[]{:S(2)}) %copy-start.4) | copy-done | bytes 3096
  26.8 0.0 copy-done.5
  26.8 0.0 copy-done.6
  26.8 16.7 %shard_map.78 = (f32[1536,128]{1,0:T(8,128)S(1)}, bf16[96,32,128]{2,1,0:T(8,128)(2,1)S(1)}, s32[832]{0:T(1024)S(1)}, s32[1]{0:T(128)}) custom-call(f32[3,6,2048]{2,1,0:T(8,128)S(1)} %copy-done.1, f32[768,128]{1,0:T(8,128)S(1)} %get-tuple-element.9.full_ref, s32[4,96]{1,0:T(4,128)S(1)} %bitcast.14, s32[8,96]{1,0:T(8,128)S(1)} %bitcast.13, s32[96]{0:T(128)S(1)} %bitcast.15), custom_call_target="tpu_custom_call" | custom-call | flops 2000000000 | bytes 4194304 | tf_op jit(solution)/shard_map/pallas_call | solution.py:289
  43.6 0.8 %all-to-all-done = f32[32,1,4608]{2,1,0:T(1,128)S(1)} async-done(((f32[32,1,4608]{2,1,0:T(1,128)}), f32[32,1,4608]{2,1,0:T(1,128)S(1)}, u32[]{:S(2)}, u32[]{:S(2)}) %all-to-all-start) | async-done | bytes 589856 | tf_op jit(solution)/shard_map/all_to_all | solution.py:282
  44.3 19.3 %shard_map.79 = (f32[3,6,2048]{2,1,0:T(8,128)}, f32[3,6,2048]{2,1,0:T(8,128)}) custom-call(f32[3,6,2048]{2,1,0:T(8,128)S(1)} %copy-done.1, f32[1152,128]{1,0:T(8,128)S(1)} %bitcast.11, bf16[96,32,128]{2,1,0:T(8,128)(2,1)S(1)} %get-tuple-element.10.tt_ref, f32[1536,128]{1,0:T(8,128)S(1)} %get-tuple-element.11.near_acc, s32[832]{0:T(1024)S(1)} %get-tuple-element.12.item_ref, ...), custom_call_target="tpu_custom_call" | custom-call | tf_op jit(solution)/shard_map/pallas_call | solution.py:308
Async XLA Ops:
  1.3 10.7 %collective-permute-start = (f32[3,6,64]{2,1,0:T(8,128)S(1)}, f32[3,6,64]{2,1,0:T(8,128)S(1)}, u32[]{:S(2)}, u32[]{:S(2)}) collective-permute-start(f32[3,6,64]{2,1,0:T(8,128)S(1)} %slice.3), channel_id=1, source_target_pairs={{1,0},{2,1},{3,2},{4,3},{5,4},{6,5},{7,6},{8,7},{9,8},{10,9},{11,1... | collective-permute-start | bytes 13832 | tf_op jit(solution)/shard_map/ppermute | solution.py:267
  2.6 9.4 %copy-start.3 = (s32[1,1,32,6]{2,1,3,0:T(1,128)S(1)}, s32[1,1,32,6]{2,1,3,0:T(1,128)}, u32[]{:S(2)}) copy-start(s32[1,1,32,6]{2,1,3,0:T(1,128)} %param.8) | copy-start | bytes 2308
  12.1 0.9 %copy-start = (f32[3,6,2048]{2,1,0:T(8,128)S(1)}, f32[3,6,2048]{2,1,0:T(8,128)}, u32[]{:S(2)}) copy-start(f32[3,6,2048]{2,1,0:T(8,128)} %pos_ref.5) | copy-start | bytes 442372
  13.0 0.8 %copy-start.2 = (f32[6,2048]{1,0:T(8,128)S(1)}, f32[6,2048]{1,0:T(8,128)}, u32[]{:S(2)}) copy-start(f32[6,2048]{1,0:T(8,128)} %circ_ref.1) | copy-start | bytes 147460
  15.8 10.4 %copy-start.1 = (f32[3,6,2048]{2,1,0:T(8,128)S(1)}, f32[3,6,2048]{2,1,0:T(8,128)}, u32[]{:S(2)}) copy-start(f32[3,6,2048]{2,1,0:T(8,128)} %pos_ref.5) | copy-start | bytes 442372
  15.8 28.6 %all-to-all-start = ((f32[32,1,4608]{2,1,0:T(1,128)}), f32[32,1,4608]{2,1,0:T(1,128)S(1)}, u32[]{:S(2)}, u32[]{:S(2)}) async-start(f32[32,1,4608]{2,1,0:T(1,128)} %bitcast.2), calls=%async_computation | async-start | bytes 1179648 | tf_op jit(solution)/shard_map/all_to_all | solution.py:282
  26.1 0.7 %copy-start.4 = (s32[1,1,96,8]{2,3,1,0:T(8,128)S(1)}, s32[1,1,96,8]{2,3,1,0:T(8,128)}, u32[]{:S(2)}) copy-start(s32[1,1,96,8]{2,3,1,0:T(8,128)} %param.9) | copy-start | bytes 9220
  26.2 0.7 %copy-start.5 = (s32[1,1,96,4]{2,3,1,0:T(4,128)S(1)}, s32[1,1,96,4]{2,3,1,0:T(4,128)}, u32[]{:S(2)}) copy-start(s32[1,1,96,4]{2,3,1,0:T(4,128)} %param.11) | copy-start | bytes 4612
  26.2 0.7 %copy-start.6 = (s32[1,1,96]{2,1,0:T(1,128)S(1)}, s32[1,1,96]{2,1,0:T(1,128)}, u32[]{:S(2)}) copy-start(s32[1,1,96]{2,1,0:T(1,128)} %param.10) | copy-start | bytes 1156

commit v6 on v5

--- a/solution.py
+++ b/solution.py
@@ -14,7 +14,7 @@
 inflow_speed = 1.0
 inv_four_pi = 0.07957747154594767
 GROUP = 8
-STEPS = 4
+STEPS = 6
 DEPTH = 32
 SUMS = 16
 F32 = jnp.float32
@@ -50,17 +50,15 @@
     return near_rows, strength_rows
 
 
-def target_rows(point):
+def target_lines(point):
     parts = [split3(point[comp]) for comp in range(3)]
     square = point[0] * point[0] + point[1] * point[1] + point[2] * point[2]
-    one, zero = jnp.ones_like(square), jnp.zeros_like(square)
-    first, second, third = ([parts[comp][level] for comp in range(3)] for level in range(3))
-    return (
-        first + first + [one, one]
-        + second + second + [zero, zero]
-        + third + [zero] * 5
-        + first + [one] + list(split3(square)) + [zero]
-    )
+    lines = [(28 + level, row) for level, row in enumerate(split3(square))]
+    for comp in range(3):
+        first, second, third = parts[comp]
+        lines += [(comp, first), (3 + comp, first), (8 + comp, second), (11 + comp, second)]
+        lines += [(16 + comp, third), (24 + comp, first)]
+    return lines
 
 
 def fixed_rows(blocks, stage):
@@ -167,7 +165,15 @@
     acc_ref, tt_ref, item_ref, total_ref, st, ww, stage, dsc, ksc,
 ):
     tiles = rows * halves
-    for r, field in enumerate(target_rows([pos_ref[comp] for comp in range(3)])):
+    line = lax.broadcasted_iota(jnp.int32, (DEPTH, TILE), 0)
+    ones = jnp.where((line == 6) | (line == 7) | (line == 27), 1.0, 0.0)
+
+    def blank(b, _):
+        stage[pl.ds(pl.multiple_of(b * DEPTH, DEPTH), DEPTH), :] = ones
+        return 0
+
+    lax.fori_loop(0, tiles, blank, 0, unroll=8)
+    for r, field in target_lines([pos_ref[comp] for comp in range(3)]):
         for half in range(halves):
             stage[pl.ds(half * DEPTH + r, rows, halves * DEPTH), :] = field[:, half * TILE : (half + 1) * TILE]
 

time: 64 us -> 61.7 us (0.964)
  the two profiles are of different devices: /device:TPU:1 before, /device:TPU:39 now
where the time goes in v6:
time: 61.7 us; the launch traced here: 61.3 us
  Pallas kernels  36.5 us (59%)
  starting transfers between devices  20.1 us (33%)
  local copies, waits for them, and re-layouts  3.16 us (5%)
  waiting for transfers between devices  0.79 us (1%)
  between operations  0.71 us (1%)
    pallas_call x1, Pallas kernels, body(): pl.pallas_call(functools.partial(far_kernel, rows, halves, peers, cap, wi...  18.7 us
    pallas_call x1, Pallas kernels, body(): pl.pallas_call(functools.partial(near_kernel, rows, halves, near, kmax),...  15.8 us
    ppermute x1, starting transfers between devices, body(): lax.ppermute(positions[:, :, :SPAN], 'age', [(s, s - 1) for s in range(1,...  11.8 us
    all_to_all x1, starting transfers between devices, body(): lax.all_to_all(outgoing.reshape(peers, 1, width_rows * TILE), 'turb', 0,...  8.29 us
    unnamed x14, local copies, waits for them, and re-layouts  2.44 us
    pallas_call x1, Pallas kernels, body(): pl.pallas_call(functools.partial(send_kernel, rows, halves, peers, cap),...  1.94 us
  transfers between devices with their start and end apart: 2, of which 1 were waited for; matrix products, arithmetic and copies ran while one was open for 0% of the time, Pallas kernels for 26%

profile of v6, /device:TPU:39, one launch (start us, length us, event | category | flops | bytes accessed | tf_op | source)
XLA Modules:
  0.0 61.3 jit_solution(1907404018203726704)
XLA Ops:
  0.6 0.7 %slice.3 = f32[3,6,64]{2,1,0:T(8,128)S(1)} slice(f32[3,6,2048]{2,1,0:T(8,128)} %pos_ref.5), slice={[0:3], [0:6], [0:64]} | slice | bytes 9216 | tf_op jit(solution)/shard_map/slice | solution.py:273
  1.3 11.8 %collective-permute-start = (f32[3,6,64]{2,1,0:T(8,128)S(1)}, f32[3,6,64]{2,1,0:T(8,128)S(1)}, u32[]{:S(2)}, u32[]{:S(2)}) collective-permute-start(f32[3,6,64]{2,1,0:T(8,128)S(1)} %slice.3), channel_id=1, source_target_pairs={{1,0},{2,1},{3,2},{4,3},{5,4},{6,5},{7,6},{8,7},{9,8},{10,9},{11,1... | collective-permute-start | bytes 13832 | tf_op jit(solution)/shard_map/ppermute | solution.py:273
  13.2 0.0 copy-start.3
  13.2 0.8 %collective-permute-done.next_ref = f32[3,6,64]{2,1,0:T(8,128)S(1)} collective-permute-done((f32[3,6,64]{2,1,0:T(8,128)S(1)}, f32[3,6,64]{2,1,0:T(8,128)S(1)}, u32[]{:S(2)}, u32[]{:S(2)}) %collective-permute-start) | collective-permute-done | bytes 4640 | tf_op jit(solution)/shard_map/ppermute | solution.py:273
  14.0 0.0 copy-done.3
  14.0 0.0 copy-start
  14.0 0.9 %copy-done = f32[3,6,2048]{2,1,0:T(8,128)S(1)} copy-done((f32[3,6,2048]{2,1,0:T(8,128)S(1)}, f32[3,6,2048]{2,1,0:T(8,128)}, u32[]{:S(2)}) %copy-start) | copy-done | bytes 147480
  14.9 0.0 copy-start.2
  14.9 0.8 %copy-done.2 = f32[6,2048]{1,0:T(8,128)S(1)} copy-done((f32[6,2048]{1,0:T(8,128)S(1)}, f32[6,2048]{1,0:T(8,128)}, u32[]{:S(2)}) %copy-start.2) | copy-done | bytes 49176
  15.7 1.9 %shard_map.77 = (f32[1152,128]{1,0:T(8,128)}, f32[768,128]{1,0:T(8,128)S(1)}) custom-call(f32[3,6,2048]{2,1,0:T(8,128)S(1)} %copy-done, f32[6,2048]{1,0:T(8,128)S(1)} %copy-done.2, f32[3,6,64]{2,1,0:T(8,128)S(1)} %collective-permute-done.next_ref, s32[1]{0:T(128)} %bitcast.last_ref, s32[1,6,1,32]{3,2,1,0:T(1,128)S(1)} %bitcast.12), custom_call_target="tpu_custom_call" | custom-call | tf_op jit(solution)/shard_map/pallas_call | solution.py:278
  17.7 0.0 copy-start.1
  17.7 8.3 %all-to-all-start = ((f32[32,1,4608]{2,1,0:T(1,128)}), f32[32,1,4608]{2,1,0:T(1,128)S(1)}, u32[]{:S(2)}, u32[]{:S(2)}) async-start(f32[32,1,4608]{2,1,0:T(1,128)} %bitcast.2), calls=%async_computation | async-start | bytes 1179648 | tf_op jit(solution)/shard_map/all_to_all | solution.py:288
  26.0 0.0 copy-start.4
  26.0 0.0 copy-start.5
  26.0 0.0 copy-start.6
  26.0 0.0 copy-done.1
  26.0 0.6 %copy-done.4 = s32[1,1,96,8]{2,3,1,0:T(8,128)S(1)} copy-done((s32[1,1,96,8]{2,3,1,0:T(8,128)S(1)}, s32[1,1,96,8]{2,3,1,0:T(8,128)}, u32[]{:S(2)}) %copy-start.4) | copy-done | bytes 3096
  26.7 0.0 copy-done.5
  26.7 0.0 copy-done.6
  26.7 15.8 %shard_map.78 = (f32[1536,128]{1,0:T(8,128)S(1)}, bf16[96,32,128]{2,1,0:T(8,128)(2,1)S(1)}, s32[832]{0:T(1024)S(1)}, s32[1]{0:T(128)}) custom-call(f32[3,6,2048]{2,1,0:T(8,128)S(1)} %copy-done.1, f32[768,128]{1,0:T(8,128)S(1)} %get-tuple-element.9.full_ref, s32[4,96]{1,0:T(4,128)S(1)} %bitcast.14, s32[8,96]{1,0:T(8,128)S(1)} %bitcast.13, s32[96]{0:T(128)S(1)} %bitcast.15), custom_call_target="tpu_custom_call" | custom-call | flops 2000000000 | bytes 4194304 | tf_op jit(solution)/shard_map/pallas_call | solution.py:295
  42.5 0.0 all-to-all-done
  42.6 18.7 %shard_map.79 = (f32[3,6,2048]{2,1,0:T(8,128)}, f32[3,6,2048]{2,1,0:T(8,128)}) custom-call(f32[3,6,2048]{2,1,0:T(8,128)S(1)} %copy-done.1, f32[1152,128]{1,0:T(8,128)S(1)} %bitcast.11, bf16[96,32,128]{2,1,0:T(8,128)(2,1)S(1)} %get-tuple-element.10.tt_ref, f32[1536,128]{1,0:T(8,128)S(1)} %get-tuple-element.11.near_acc, s32[832]{0:T(1024)S(1)} %get-tuple-element.12.item_ref, ...), custom_call_target="tpu_custom_call" | custom-call | tf_op jit(solution)/shard_map/pallas_call | solution.py:314
Async XLA Ops:
  1.3 12.6 %collective-permute-start = (f32[3,6,64]{2,1,0:T(8,128)S(1)}, f32[3,6,64]{2,1,0:T(8,128)S(1)}, u32[]{:S(2)}, u32[]{:S(2)}) collective-permute-start(f32[3,6,64]{2,1,0:T(8,128)S(1)} %slice.3), channel_id=1, source_target_pairs={{1,0},{2,1},{3,2},{4,3},{5,4},{6,5},{7,6},{8,7},{9,8},{10,9},{11,1... | collective-permute-start | bytes 13832 | tf_op jit(solution)/shard_map/ppermute | solution.py:273
  13.2 0.8 %copy-start.3 = (s32[1,1,32,6]{2,1,3,0:T(1,128)S(1)}, s32[1,1,32,6]{2,1,3,0:T(1,128)}, u32[]{:S(2)}) copy-start(s32[1,1,32,6]{2,1,3,0:T(1,128)} %param.8) | copy-start | bytes 2308
  14.0 0.9 %copy-start = (f32[3,6,2048]{2,1,0:T(8,128)S(1)}, f32[3,6,2048]{2,1,0:T(8,128)}, u32[]{:S(2)}) copy-start(f32[3,6,2048]{2,1,0:T(8,128)} %pos_ref.5) | copy-start | bytes 442372
  14.9 0.8 %copy-start.2 = (f32[6,2048]{1,0:T(8,128)S(1)}, f32[6,2048]{1,0:T(8,128)}, u32[]{:S(2)}) copy-start(f32[6,2048]{1,0:T(8,128)} %circ_ref.1) | copy-start | bytes 147460
  17.7 8.3 %copy-start.1 = (f32[3,6,2048]{2,1,0:T(8,128)S(1)}, f32[3,6,2048]{2,1,0:T(8,128)}, u32[]{:S(2)}) copy-start(f32[3,6,2048]{2,1,0:T(8,128)} %pos_ref.5) | copy-start | bytes 442372
  17.7 24.9 %all-to-all-start = ((f32[32,1,4608]{2,1,0:T(1,128)}), f32[32,1,4608]{2,1,0:T(1,128)S(1)}, u32[]{:S(2)}, u32[]{:S(2)}) async-start(f32[32,1,4608]{2,1,0:T(1,128)} %bitcast.2), calls=%async_computation | async-start | bytes 1179648 | tf_op jit(solution)/shard_map/all_to_all | solution.py:288
  26.0 0.7 %copy-start.4 = (s32[1,1,96,8]{2,3,1,0:T(8,128)S(1)}, s32[1,1,96,8]{2,3,1,0:T(8,128)}, u32[]{:S(2)}) copy-start(s32[1,1,96,8]{2,3,1,0:T(8,128)} %param.9) | copy-start | bytes 9220
  26.0 0.7 %copy-start.5 = (s32[1,1,96,4]{2,3,1,0:T(4,128)S(1)}, s32[1,1,96,4]{2,3,1,0:T(4,128)}, u32[]{:S(2)}) copy-start(s32[1,1,96,4]{2,3,1,0:T(4,128)} %param.11) | copy-start | bytes 4612
  26.0 0.7 %copy-start.6 = (s32[1,1,96]{2,1,0:T(1,128)S(1)}, s32[1,1,96]{2,1,0:T(1,128)}, u32[]{:S(2)}) copy-start(s32[1,1,96]{2,1,0:T(1,128)} %param.10) | copy-start | bytes 1156

commit v7 on v6

--- a/solution.py
+++ b/solution.py
@@ -89,26 +89,47 @@
     return list(enumerate(near_rows)) + [(16 + r, row) for r, row in enumerate(strength_rows)]
 
 
-def send_kernel(
-    rows, halves, peers, cap, pos_ref, circ_ref, next_ref, last_ref, list_ref, out_ref, full_ref
-):
+def left_half(rows):
+    return lax.broadcasted_iota(jnp.int32, (rows, TILE), 1) < SPAN
+
+
+def lattice(here, beyond, circ):
+    first = left_half(circ.shape[0])
+    middles, strengths = [], []
+    for comp in range(3):
+        following = jnp.where(first, pltpu.roll(here[comp], SPAN, 1), beyond[comp])
+        segment = following - here[comp]
+        middles.append(here[comp] + 0.5 * segment)
+        strengths.append(circ * segment)
+    return middles, strengths
+
+
+def send_kernel(rows, halves, peers, cap, pos_ref, circ_ref, next_ref, last_ref, list_ref, out_ref, full_ref):
     ends = last_ref[0] == 1
-    for comp in range(3):
-        here = pos_ref[comp]
-        beyond = jnp.where(ends, here[:, -SPAN:], next_ref[comp])
-        segment = jnp.concatenate([here[:, SPAN:], beyond], axis=1) - here
-        middle = here + 0.5 * segment
-        strength = circ_ref[...] * segment
-        for half in range(halves):
-            cut = slice(half * TILE, (half + 1) * TILE)
-            full_ref[pl.ds(half * 8 + comp, rows, halves * 8), :] = middle[:, cut]
-            full_ref[pl.ds(half * 8 + 3 + comp, rows, halves * 8), :] = strength[:, cut]
+    width = halves * TILE
+    for half in range(halves):
+        cut = slice(half * TILE, (half + 1) * TILE)
+        full_ref[pl.ds(half * 8 + 3, rows, halves * 8), :] = circ_ref[:, cut]
+        for comp in range(3):
+            full_ref[pl.ds(half * 8 + comp, rows, halves * 8), :] = pos_ref[comp, :, cut]
+            if half == halves - 1:
+                after = jnp.where(ends, pos_ref[comp, :, width - SPAN :], next_ref[comp])
+            else:
+                after = pos_ref[comp, :, (half + 1) * TILE : (half + 1) * TILE + SPAN]
+            full_ref[pl.ds(half * 8 + 4 + comp, rows, halves * 8), :] = jnp.concatenate([after, after], axis=1)
+    first = left_half(3)
 
     def fill(peer, _):
+        base = peer * (cap * 11 // 2)
+        after = None
         for c in range(cap):
             block = list_ref[0, c, 0, peer]
             data = full_ref[pl.ds(pl.multiple_of(block * 8, 8), 8), :]
-            out_ref[pl.ds(peer * (cap * 6) + c * 6, 6), :] = data[:6]
+            out_ref[pl.ds(base + c * 4, 4), :] = data[:4]
+            if c % 2 == 0:
+                after = data[4:7]
+            else:
+                out_ref[pl.ds(base + cap * 4 + c // 2 * 3, 3), :] = jnp.where(first, after, data[4:7])
         return 0
 
     lax.fori_loop(0, peers, fill, 0, unroll=2)
@@ -195,8 +216,8 @@
 
     fixed_rows(tiles, stage)
     for half in range(halves):
-        parts = [full_ref[pl.ds(half * 8 + comp, rows, halves * 8), :] for comp in range(6)]
-        for r, field in source_lines(*source_rows(parts[:3], parts[3:])):
+        parts = [full_ref[pl.ds(half * 8 + line, rows, halves * 8), :] for line in range(7)]
+        for r, field in source_lines(*source_rows(*lattice(parts[:3], parts[4:], parts[3]))):
             stage[pl.ds(half * DEPTH + r, rows, halves * DEPTH), :] = field
     pack_sources(tiles, stage, st, ww)
     last = tiles * near - 1
@@ -220,10 +241,11 @@
 
     def lay(group, _):
         for c in range(cap):
-            parts = [
-                recv_ref[pl.ds(group * (8 * width_rows) + c * 6 + comp, 8, width_rows), :] for comp in range(6)
-            ]
-            for r, field in source_lines(*source_rows(parts[:3], parts[3:])):
+            base = group * (8 * width_rows)
+            lines = [c * 4 + line for line in range(4)] + [cap * 4 + c // 2 * 3 + comp for comp in range(3)]
+            parts = [recv_ref[pl.ds(base + line, 8, width_rows), :] for line in lines]
+            beyond = parts[4:] if c % 2 else [pltpu.roll(part, SPAN, 1) for part in parts[4:]]
+            for r, field in source_lines(*source_rows(*lattice(parts[:3], beyond, parts[3]))):
                 stage[pl.ds(group * (8 * cap * DEPTH) + c * DEPTH + r, 8, cap * DEPTH), :] = field
         return 0
 
@@ -272,7 +294,7 @@
     ages = lax.axis_size("age")
     next_row = lax.ppermute(positions[:, :, :SPAN], "age", [(s, s - 1) for s in range(1, ages)])
     last = (lax.axis_index("age") == ages - 1).astype(jnp.int32).reshape(1)
-    width_rows = cap * 6
+    width_rows = cap * 11 // 2
     params = pltpu.CompilerParams(vmem_limit_bytes=48 << 20)
 
     outgoing, full = pl.pallas_call(

time: 61.7 us -> 62.4 us (1.011)
  the two profiles are of different devices: /device:TPU:39 before, /device:TPU:3 now
where the time goes in v7:
time: 62.4 us; the launch traced here: 62 us
  Pallas kernels  36.7 us (59%)
  starting transfers between devices  20.1 us (32%)
  local copies, waits for them, and re-layouts  3.16 us (5%)
  waiting for transfers between devices  1.37 us (2%)
  between operations  0.7 us (1%)
    pallas_call x1, Pallas kernels, body(): pl.pallas_call(functools.partial(far_kernel, rows, halves, peers, cap, wi...  19 us
    pallas_call x1, Pallas kernels, body(): pl.pallas_call(functools.partial(near_kernel, rows, halves, near, kmax),...  15.9 us
    ppermute x1, starting transfers between devices, body(): lax.ppermute(positions[:, :, :SPAN], 'age', [(s, s - 1) for s in range(1,...  12.4 us
    all_to_all x1, starting transfers between devices, body(): lax.all_to_all(outgoing.reshape(peers, 1, width_rows * TILE), 'turb', 0,...  7.65 us
    unnamed x14, local copies, waits for them, and re-layouts  2.44 us
    pallas_call x1, Pallas kernels, body(): pl.pallas_call(functools.partial(send_kernel, rows, halves, peers, cap),...  1.92 us
  transfers between devices with their start and end apart: 2, of which 2 were waited for; matrix products, arithmetic and copies ran while one was open for 0% of the time, Pallas kernels for 26%

profile of v7, /device:TPU:3, one launch (start us, length us, event | category | flops | bytes accessed | tf_op | source)
XLA Modules:
  0.0 62.0 jit_solution(16490686575062321410)
XLA Ops:
  0.6 0.7 %slice.3 = f32[3,6,64]{2,1,0:T(8,128)S(1)} slice(f32[3,6,2048]{2,1,0:T(8,128)} %pos_ref.5), slice={[0:3], [0:6], [0:64]} | slice | bytes 9216 | tf_op jit(solution)/shard_map/slice | solution.py:295
  1.3 12.4 %collective-permute-start = (f32[3,6,64]{2,1,0:T(8,128)S(1)}, f32[3,6,64]{2,1,0:T(8,128)S(1)}, u32[]{:S(2)}, u32[]{:S(2)}) collective-permute-start(f32[3,6,64]{2,1,0:T(8,128)S(1)} %slice.3), channel_id=1, source_target_pairs={{1,0},{2,1},{3,2},{4,3},{5,4},{6,5},{7,6},{8,7},{9,8},{10,9},{11,1... | collective-permute-start | bytes 13832 | tf_op jit(solution)/shard_map/ppermute | solution.py:295
  13.8 0.0 copy-start.3
  13.8 0.8 %collective-permute-done.next_ref = f32[3,6,64]{2,1,0:T(8,128)S(1)} collective-permute-done((f32[3,6,64]{2,1,0:T(8,128)S(1)}, f32[3,6,64]{2,1,0:T(8,128)S(1)}, u32[]{:S(2)}, u32[]{:S(2)}) %collective-permute-start) | collective-permute-done | bytes 4640 | tf_op jit(solution)/shard_map/ppermute | solution.py:295
  14.6 0.0 copy-done.3
  14.6 0.0 copy-start
  14.6 0.9 %copy-done = f32[3,6,2048]{2,1,0:T(8,128)S(1)} copy-done((f32[3,6,2048]{2,1,0:T(8,128)S(1)}, f32[3,6,2048]{2,1,0:T(8,128)}, u32[]{:S(2)}) %copy-start) | copy-done | bytes 147480
  15.5 0.0 copy-start.2
  15.5 0.8 %copy-done.2 = f32[6,2048]{1,0:T(8,128)S(1)} copy-done((f32[6,2048]{1,0:T(8,128)S(1)}, f32[6,2048]{1,0:T(8,128)}, u32[]{:S(2)}) %copy-start.2) | copy-done | bytes 49176
  16.4 1.9 %shard_map.77 = (f32[1056,128]{1,0:T(8,128)}, f32[768,128]{1,0:T(8,128)S(1)}) custom-call(f32[3,6,2048]{2,1,0:T(8,128)S(1)} %copy-done, f32[6,2048]{1,0:T(8,128)S(1)} %copy-done.2, f32[3,6,64]{2,1,0:T(8,128)S(1)} %collective-permute-done.next_ref, s32[1]{0:T(128)} %bitcast.last_ref, s32[1,6,1,32]{3,2,1,0:T(1,128)S(1)} %bitcast.12), custom_call_target="tpu_custom_call" | custom-call | tf_op jit(solution)/shard_map/pallas_call | solution.py:300
  18.3 0.0 copy-start.1
  18.3 7.6 %all-to-all-start = ((f32[32,1,4224]{2,1,0:T(1,128)}), f32[32,1,4224]{2,1,0:T(1,128)S(1)}, u32[]{:S(2)}, u32[]{:S(2)}) async-start(f32[32,1,4224]{2,1,0:T(1,128)} %bitcast.2), calls=%async_computation | async-start | bytes 1081344 | tf_op jit(solution)/shard_map/all_to_all | solution.py:310
  25.9 0.0 copy-start.4
  25.9 0.0 copy-start.5
  25.9 0.0 copy-start.6
  26.0 0.0 copy-done.1
  26.0 0.6 %copy-done.4 = s32[1,1,96,8]{2,3,1,0:T(8,128)S(1)} copy-done((s32[1,1,96,8]{2,3,1,0:T(8,128)S(1)}, s32[1,1,96,8]{2,3,1,0:T(8,128)}, u32[]{:S(2)}) %copy-start.4) | copy-done | bytes 3096
  26.6 0.0 copy-done.5
  26.6 0.0 copy-done.6
  26.6 15.9 %shard_map.78 = (f32[1536,128]{1,0:T(8,128)S(1)}, bf16[96,32,128]{2,1,0:T(8,128)(2,1)S(1)}, s32[832]{0:T(1024)S(1)}, s32[1]{0:T(128)}) custom-call(f32[3,6,2048]{2,1,0:T(8,128)S(1)} %copy-done.1, f32[768,128]{1,0:T(8,128)S(1)} %get-tuple-element.9.full_ref, s32[4,96]{1,0:T(4,128)S(1)} %bitcast.14, s32[8,96]{1,0:T(8,128)S(1)} %bitcast.13, s32[96]{0:T(128)S(1)} %bitcast.15), custom_call_target="tpu_custom_call" | custom-call | flops 2000000000 | bytes 4194304 | tf_op jit(solution)/shard_map/pallas_call | solution.py:317
  42.5 0.6 all-to-all-done
  43.1 19.0 %shard_map.79 = (f32[3,6,2048]{2,1,0:T(8,128)}, f32[3,6,2048]{2,1,0:T(8,128)}) custom-call(f32[3,6,2048]{2,1,0:T(8,128)S(1)} %copy-done.1, f32[1056,128]{1,0:T(8,128)S(1)} %bitcast.11, bf16[96,32,128]{2,1,0:T(8,128)(2,1)S(1)} %get-tuple-element.10.tt_ref, f32[1536,128]{1,0:T(8,128)S(1)} %get-tuple-element.11.near_acc, s32[832]{0:T(1024)S(1)} %get-tuple-element.12.item_ref, ...), custom_call_target="tpu_custom_call" | custom-call | tf_op jit(solution)/shard_map/pallas_call | solution.py:336
Async XLA Ops:
  1.3 13.2 %collective-permute-start = (f32[3,6,64]{2,1,0:T(8,128)S(1)}, f32[3,6,64]{2,1,0:T(8,128)S(1)}, u32[]{:S(2)}, u32[]{:S(2)}) collective-permute-start(f32[3,6,64]{2,1,0:T(8,128)S(1)} %slice.3), channel_id=1, source_target_pairs={{1,0},{2,1},{3,2},{4,3},{5,4},{6,5},{7,6},{8,7},{9,8},{10,9},{11,1... | collective-permute-start | bytes 13832 | tf_op jit(solution)/shard_map/ppermute | solution.py:295
  13.8 0.8 %copy-start.3 = (s32[1,1,32,6]{2,1,3,0:T(1,128)S(1)}, s32[1,1,32,6]{2,1,3,0:T(1,128)}, u32[]{:S(2)}) copy-start(s32[1,1,32,6]{2,1,3,0:T(1,128)} %param.8) | copy-start | bytes 2308
  14.6 0.9 %copy-start = (f32[3,6,2048]{2,1,0:T(8,128)S(1)}, f32[3,6,2048]{2,1,0:T(8,128)}, u32[]{:S(2)}) copy-start(f32[3,6,2048]{2,1,0:T(8,128)} %pos_ref.5) | copy-start | bytes 442372
  15.5 0.8 %copy-start.2 = (f32[6,2048]{1,0:T(8,128)S(1)}, f32[6,2048]{1,0:T(8,128)}, u32[]{:S(2)}) copy-start(f32[6,2048]{1,0:T(8,128)} %circ_ref.1) | copy-start | bytes 147460
  18.3 7.7 %copy-start.1 = (f32[3,6,2048]{2,1,0:T(8,128)S(1)}, f32[3,6,2048]{2,1,0:T(8,128)}, u32[]{:S(2)}) copy-start(f32[3,6,2048]{2,1,0:T(8,128)} %pos_ref.5) | copy-start | bytes 442372
  18.3 24.8 %all-to-all-start = ((f32[32,1,4224]{2,1,0:T(1,128)}), f32[32,1,4224]{2,1,0:T(1,128)S(1)}, u32[]{:S(2)}, u32[]{:S(2)}) async-start(f32[32,1,4224]{2,1,0:T(1,128)} %bitcast.2), calls=%async_computation | async-start | bytes 1081344 | tf_op jit(solution)/shard_map/all_to_all | solution.py:310
  25.9 0.7 %copy-start.4 = (s32[1,1,96,8]{2,3,1,0:T(8,128)S(1)}, s32[1,1,96,8]{2,3,1,0:T(8,128)}, u32[]{:S(2)}) copy-start(s32[1,1,96,8]{2,3,1,0:T(8,128)} %param.9) | copy-start | bytes 9220
  25.9 0.7 %copy-start.5 = (s32[1,1,96,4]{2,3,1,0:T(4,128)S(1)}, s32[1,1,96,4]{2,3,1,0:T(4,128)}, u32[]{:S(2)}) copy-start(s32[1,1,96,4]{2,3,1,0:T(4,128)} %param.11) | copy-start | bytes 4612
  25.9 0.7 %copy-start.6 = (s32[1,1,96]{2,1,0:T(1,128)S(1)}, s32[1,1,96]{2,1,0:T(1,128)}, u32[]{:S(2)}) copy-start(s32[1,1,96]{2,1,0:T(1,128)} %param.10) | copy-start | bytes 1156

commit v8 on v7

--- a/solution.py
+++ b/solution.py
@@ -170,15 +170,20 @@
     kernels(0)
     distances(1, 1)
 
-    def turn(index, _):
-        for h in range(STEPS):
-            step, side = index * STEPS + h, h % 2
-            gather(step, side)
-            kernels(1 - side)
-            distances(step + 2, side)
-        return 0
-
-    lax.fori_loop(0, count, turn, 0)
+    def turns(first, times, length):
+        def turn(index, _):
+            for h in range(length):
+                step, side = first + index * length + h, h % 2
+                gather(step, side)
+                kernels(1 - side)
+                distances(step + 2, side)
+            return 0
+
+        lax.fori_loop(0, times, turn, 0)
+
+    whole = lax.div(count, STEPS // 2)
+    turns(0, whole, STEPS)
+    turns(whole * STEPS, count - whole * (STEPS // 2), 2)
 
 
 def near_kernel(
@@ -228,7 +233,7 @@
         return b, near_ref[i - b * near, b]
 
     acc_ref[...] = jnp.zeros_like(acc_ref)
-    interact(tiles * near // (STEPS * GROUP), item, tt_ref, st, ww, acc_ref, dsc, ksc)
+    interact(-(-tiles * near // (2 * GROUP)), item, tt_ref, st, ww, acc_ref, dsc, ksc)
 
 
 def far_kernel(
@@ -257,8 +262,8 @@
         return lax.shift_right_logical(code, 8), lax.bitwise_and(code, 255)
 
     acc[: rows * halves * SUMS, :] = near_acc[...]
-    turns = lax.div(total_ref[0] + STEPS * GROUP - 1, STEPS * GROUP)
-    interact(turns, item, tt_ref, st, ww, acc, dsc, ksc)
+    pairs = lax.div(total_ref[0] + 2 * GROUP - 1, 2 * GROUP)
+    interact(pairs, item, tt_ref, st, ww, acc, dsc, ksc)
 
     for half in range(halves):
         cut = slice(half * TILE, (half + 1) * TILE)

time: 62.4 us -> 62.1 us (level)
  the two profiles are of different devices: /device:TPU:3 before, /device:TPU:15 now
where the time goes in v8:
time: 62.1 us; the launch traced here: 61.7 us
  Pallas kernels  36.6 us (59%)
  starting transfers between devices  20.4 us (33%)
  local copies, waits for them, and re-layouts  3.16 us (5%)
  waiting for transfers between devices  0.79 us (1%)
  between operations  0.71 us (1%)
    pallas_call x1, Pallas kernels, body(): pl.pallas_call(functools.partial(far_kernel, rows, halves, peers, cap, wi...  18.8 us
    pallas_call x1, Pallas kernels, body(): pl.pallas_call(functools.partial(near_kernel, rows, halves, near, kmax),...  15.9 us
    ppermute x1, starting transfers between devices, body(): lax.ppermute(positions[:, :, :SPAN], 'age', [(s, s - 1) for s in range(1,...  12.7 us
    all_to_all x1, starting transfers between devices, body(): lax.all_to_all(outgoing.reshape(peers, 1, width_rows * TILE), 'turb', 0,...  7.74 us
    unnamed x14, local copies, waits for them, and re-layouts  2.44 us
    pallas_call x1, Pallas kernels, body(): pl.pallas_call(functools.partial(send_kernel, rows, halves, peers, cap),...  1.92 us
  transfers between devices with their start and end apart: 2, of which 1 were waited for; matrix products, arithmetic and copies ran while one was open for 0% of the time, Pallas kernels for 26%

profile of v8, /device:TPU:15, one launch (start us, length us, event | category | flops | bytes accessed | tf_op | source)
XLA Modules:
  0.0 61.7 jit_solution(12147126898067014301)
XLA Ops:
  0.6 0.7 %slice.3 = f32[3,6,64]{2,1,0:T(8,128)S(1)} slice(f32[3,6,2048]{2,1,0:T(8,128)} %pos_ref.5), slice={[0:3], [0:6], [0:64]} | slice | bytes 9216 | tf_op jit(solution)/shard_map/slice | solution.py:300
  1.3 12.7 %collective-permute-start = (f32[3,6,64]{2,1,0:T(8,128)S(1)}, f32[3,6,64]{2,1,0:T(8,128)S(1)}, u32[]{:S(2)}, u32[]{:S(2)}) collective-permute-start(f32[3,6,64]{2,1,0:T(8,128)S(1)} %slice.3), channel_id=1, source_target_pairs={{1,0},{2,1},{3,2},{4,3},{5,4},{6,5},{7,6},{8,7},{9,8},{10,9},{11,1... | collective-permute-start | bytes 13832 | tf_op jit(solution)/shard_map/ppermute | solution.py:300
  14.1 0.0 copy-start.3
  14.1 0.8 %collective-permute-done.next_ref = f32[3,6,64]{2,1,0:T(8,128)S(1)} collective-permute-done((f32[3,6,64]{2,1,0:T(8,128)S(1)}, f32[3,6,64]{2,1,0:T(8,128)S(1)}, u32[]{:S(2)}, u32[]{:S(2)}) %collective-permute-start) | collective-permute-done | bytes 4640 | tf_op jit(solution)/shard_map/ppermute | solution.py:300
  14.9 0.0 copy-done.3
  14.9 0.0 copy-start
  14.9 0.9 %copy-done = f32[3,6,2048]{2,1,0:T(8,128)S(1)} copy-done((f32[3,6,2048]{2,1,0:T(8,128)S(1)}, f32[3,6,2048]{2,1,0:T(8,128)}, u32[]{:S(2)}) %copy-start) | copy-done | bytes 147480
  15.8 0.0 copy-start.2
  15.8 0.8 %copy-done.2 = f32[6,2048]{1,0:T(8,128)S(1)} copy-done((f32[6,2048]{1,0:T(8,128)S(1)}, f32[6,2048]{1,0:T(8,128)}, u32[]{:S(2)}) %copy-start.2) | copy-done | bytes 49176
  16.6 1.9 %shard_map.77 = (f32[1056,128]{1,0:T(8,128)}, f32[768,128]{1,0:T(8,128)S(1)}) custom-call(f32[3,6,2048]{2,1,0:T(8,128)S(1)} %copy-done, f32[6,2048]{1,0:T(8,128)S(1)} %copy-done.2, f32[3,6,64]{2,1,0:T(8,128)S(1)} %collective-permute-done.next_ref, s32[1]{0:T(128)} %bitcast.last_ref, s32[1,6,1,32]{3,2,1,0:T(1,128)S(1)} %bitcast.12), custom_call_target="tpu_custom_call" | custom-call | tf_op jit(solution)/shard_map/pallas_call | solution.py:305
  18.6 0.0 copy-start.1
  18.6 7.7 %all-to-all-start = ((f32[32,1,4224]{2,1,0:T(1,128)}), f32[32,1,4224]{2,1,0:T(1,128)S(1)}, u32[]{:S(2)}, u32[]{:S(2)}) async-start(f32[32,1,4224]{2,1,0:T(1,128)} %bitcast.2), calls=%async_computation | async-start | bytes 1081344 | tf_op jit(solution)/shard_map/all_to_all | solution.py:315
  26.3 0.0 copy-start.4
  26.3 0.0 copy-start.5
  26.3 0.0 copy-start.6
  26.3 0.0 copy-done.1
  26.4 0.6 %copy-done.4 = s32[1,1,96,8]{2,3,1,0:T(8,128)S(1)} copy-done((s32[1,1,96,8]{2,3,1,0:T(8,128)S(1)}, s32[1,1,96,8]{2,3,1,0:T(8,128)}, u32[]{:S(2)}) %copy-start.4) | copy-done | bytes 3096
  27.0 0.0 copy-done.5
  27.0 0.0 copy-done.6
  27.0 15.9 %shard_map.78 = (f32[1536,128]{1,0:T(8,128)S(1)}, bf16[96,32,128]{2,1,0:T(8,128)(2,1)S(1)}, s32[832]{0:T(1024)S(1)}, s32[1]{0:T(128)}) custom-call(f32[3,6,2048]{2,1,0:T(8,128)S(1)} %copy-done.1, f32[768,128]{1,0:T(8,128)S(1)} %get-tuple-element.9.full_ref, s32[4,96]{1,0:T(4,128)S(1)} %bitcast.14, s32[8,96]{1,0:T(8,128)S(1)} %bitcast.13, s32[96]{0:T(128)S(1)} %bitcast.15), custom_call_target="tpu_custom_call" | custom-call | flops 2000000000 | bytes 4194304 | tf_op jit(solution)/shard_map/pallas_call | solution.py:322
  42.9 0.0 all-to-all-done
  42.9 18.8 %shard_map.79 = (f32[3,6,2048]{2,1,0:T(8,128)}, f32[3,6,2048]{2,1,0:T(8,128)}) custom-call(f32[3,6,2048]{2,1,0:T(8,128)S(1)} %copy-done.1, f32[1056,128]{1,0:T(8,128)S(1)} %bitcast.11, bf16[96,32,128]{2,1,0:T(8,128)(2,1)S(1)} %get-tuple-element.10.tt_ref, f32[1536,128]{1,0:T(8,128)S(1)} %get-tuple-element.11.near_acc, s32[832]{0:T(1024)S(1)} %get-tuple-element.12.item_ref, ...), custom_call_target="tpu_custom_call" | custom-call | tf_op jit(solution)/shard_map/pallas_call | solution.py:341
Async XLA Ops:
  1.3 13.5 %collective-permute-start = (f32[3,6,64]{2,1,0:T(8,128)S(1)}, f32[3,6,64]{2,1,0:T(8,128)S(1)}, u32[]{:S(2)}, u32[]{:S(2)}) collective-permute-start(f32[3,6,64]{2,1,0:T(8,128)S(1)} %slice.3), channel_id=1, source_target_pairs={{1,0},{2,1},{3,2},{4,3},{5,4},{6,5},{7,6},{8,7},{9,8},{10,9},{11,1... | collective-permute-start | bytes 13832 | tf_op jit(solution)/shard_map/ppermute | solution.py:300
  14.1 0.8 %copy-start.3 = (s32[1,1,32,6]{2,1,3,0:T(1,128)S(1)}, s32[1,1,32,6]{2,1,3,0:T(1,128)}, u32[]{:S(2)}) copy-start(s32[1,1,32,6]{2,1,3,0:T(1,128)} %param.8) | copy-start | bytes 2308
  14.9 0.9 %copy-start = (f32[3,6,2048]{2,1,0:T(8,128)S(1)}, f32[3,6,2048]{2,1,0:T(8,128)}, u32[]{:S(2)}) copy-start(f32[3,6,2048]{2,1,0:T(8,128)} %pos_ref.5) | copy-start | bytes 442372
  15.8 0.8 %copy-start.2 = (f32[6,2048]{1,0:T(8,128)S(1)}, f32[6,2048]{1,0:T(8,128)}, u32[]{:S(2)}) copy-start(f32[6,2048]{1,0:T(8,128)} %circ_ref.1) | copy-start | bytes 147460
  18.6 7.8 %copy-start.1 = (f32[3,6,2048]{2,1,0:T(8,128)S(1)}, f32[3,6,2048]{2,1,0:T(8,128)}, u32[]{:S(2)}) copy-start(f32[3,6,2048]{2,1,0:T(8,128)} %pos_ref.5) | copy-start | bytes 442372
  18.6 24.3 %all-to-all-start = ((f32[32,1,4224]{2,1,0:T(1,128)}), f32[32,1,4224]{2,1,0:T(1,128)S(1)}, u32[]{:S(2)}, u32[]{:S(2)}) async-start(f32[32,1,4224]{2,1,0:T(1,128)} %bitcast.2), calls=%async_computation | async-start | bytes 1081344 | tf_op jit(solution)/shard_map/all_to_all | solution.py:315
  26.3 0.7 %copy-start.4 = (s32[1,1,96,8]{2,3,1,0:T(8,128)S(1)}, s32[1,1,96,8]{2,3,1,0:T(8,128)}, u32[]{:S(2)}) copy-start(s32[1,1,96,8]{2,3,1,0:T(8,128)} %param.9) | copy-start | bytes 9220
  26.3 0.7 %copy-start.5 = (s32[1,1,96,4]{2,3,1,0:T(4,128)S(1)}, s32[1,1,96,4]{2,3,1,0:T(4,128)}, u32[]{:S(2)}) copy-start(s32[1,1,96,4]{2,3,1,0:T(4,128)} %param.11) | copy-start | bytes 4612
  26.3 0.7 %copy-start.6 = (s32[1,1,96]{2,1,0:T(1,128)S(1)}, s32[1,1,96]{2,1,0:T(1,128)}, u32[]{:S(2)}) copy-start(s32[1,1,96]{2,1,0:T(1,128)} %param.10) | copy-start | bytes 1156
